TPU v7x, 128 devices: a whole 4x4x4 slice. The times are simulated.
128 devices in a mesh: bx: 8 (over z, x_hi), by: 16 (over y, x_lo, core).
Axes of the slice: x: 4 (x_hi: 2, x_lo: 2; x = x_hi * 2 + x_lo), y: 4, z: 4, core: 2. Of those that a mesh axis runs over, the one named last changes fastest.
Arguments:
- latent: bfloat16 [65536, 128], P(('bx', 'by')), may hold values from -6 to 6
- move_to: int32 [65536], P(('bx', 'by')), may hold values from 0 to 8, as said below
- move_slot: int32 [65536], P(('bx', 'by')), may hold values from 0 to 511, as said below
- arrive_from: int32 [65536], P(('bx', 'by')), may hold values from 0 to 8, as said below
- arrive_slot: int32 [65536], P(('bx', 'by')), may hold values from 0 to 511, as said below
- neighbours: int32 [65536, 16], P(('bx', 'by')), may hold values from 0 to 831
- valid_count: int32 [65536], P(('bx', 'by')), may hold values from 1 to 16
- face_send: int32 [8, 16, 4, 64], P('bx', 'by'), may hold values from 0 to 511
- corner_send: int32 [8, 16, 4, 16], P('bx', 'by'), may hold values from 0 to 511
- edge_in: bfloat16 [2, 2, 128, 128], replicated, may hold values from -0.375 to 0.375
- edge_hid: bfloat16 [2, 2, 128, 128], replicated, may hold values from -0.5 to 0.5
- node_in: bfloat16 [2, 2, 128, 128], replicated, may hold values from -0.375 to 0.375
- node_out: bfloat16 [2, 128, 128], replicated, may hold values from -0.5 to 0.5
- biases: float32 [2, 5, 128], replicated, may hold values from -2 to 2
- gains: float32 [2, 2, 128], replicated, may hold values from 0.5 to 1.5
- grad_out: bfloat16 [65536, 128], P(('bx', 'by')), may hold values from -0.59765625 to 0.59765625
Outputs:
- latent_out: bfloat16 [65536, 128], P(('bx', 'by'))
- grad_latent: bfloat16 [65536, 128], P(('bx', 'by'))
- grad_edge_in: float32 [2, 2, 128, 128], replicated
- grad_edge_hid: float32 [2, 2, 128, 128], replicated
- grad_node_in: float32 [2, 2, 128, 128], replicated
- grad_node_out: float32 [2, 128, 128], replicated
- grad_biases: float32 [2, 5, 128], replicated
- grad_gains: float32 [2, 2, 128], replicated
Inputs may be any that keep to these rules, and one draw needn't show every extreme that they name: `move_to`: each particle's direction code of migration; codes other than 4 go to one of the eight bins around. `move_slot`: for a moving particle its slot in the list of its device and direction, 0 to 31, distinct within that list and filling it from 0; for a staying particle its row on the same device after migration. `arrive_from`: for each row after migration the direction code by which it came; with move_to and move_slot the lists describe one permutation of all particles. One device hands at most 32 particles to one neighbour, and some device hands exactly 32 in every draw. `arrive_slot`: for an arrived row its slot in the sender's list for that direction; for a staying row its old row on the same device.
All inputs are finite; a program needn't handle non-finite values.
Results may differ from a plain program's by a relative error of at most 0.025.
Values may be sent and summed in bfloat16 or wider, within the bound.
A program may use at most 128 MiB of HBM per device.

v0:
```python
from functools import partial
import math

import jax
import jax.numpy as jnp
from jax import lax
from jax.sharding import PartitionSpec as P

LAYERS = 2
CAP = 32


def from_behind(value, axis, steps):
    count = lax.axis_size(axis)
    pairs = [(source, (source + steps) % count) for source in range(count)]
    return lax.ppermute(value, axis, pairs)


def layer_norm(values, gain):
    average = jnp.mean(values, axis=-1, keepdims=True)
    centred = values - average
    variance = jnp.mean(jnp.square(centred), axis=-1, keepdims=True)
    return centred * lax.rsqrt(variance + 1e-05) * gain


def pick_rows(index, source):
    hits = (index[:, None] == jnp.arange(source.shape[0], dtype=jnp.int32)[None, :]).astype(
        source.dtype
    )
    return jnp.dot(hits, source, preferred_element_type=jnp.float32).astype(source.dtype)


def fill_slots(target, source, count):
    hits = (jnp.arange(count, dtype=jnp.int32)[:, None] == target[None, :]).astype(source.dtype)
    return jnp.dot(hits, source, preferred_element_type=jnp.float32).astype(source.dtype)


def split_pair(values):
    high = values.astype(jnp.bfloat16)
    low = (values - high.astype(jnp.float32)).astype(jnp.bfloat16)
    return jnp.concatenate([high, low], axis=1)


def place_rows(index, values, row_count):
    width = values.shape[1]
    hits = (jnp.arange(row_count, dtype=jnp.int32)[:, None] == index[None, :]).astype(jnp.bfloat16)
    both = jnp.dot(hits, split_pair(values), preferred_element_type=jnp.float32)
    return both[:, :width] + both[:, width:]


def edge_block(
    receiver_part, sender_part, count_block, w_mid, w_out, bias_in, bias_mid, bias_out, edge_gain
):
    width = receiver_part.shape[-1]
    fanout = sender_part.shape[1]
    pre_act = receiver_part[:, None, :] + sender_part + bias_in
    hidden_one = jax.nn.silu(pre_act).astype(jnp.bfloat16).reshape(-1, width)
    hidden_two = jax.nn.silu(
        jnp.dot(hidden_one, w_mid, preferred_element_type=jnp.float32) + bias_mid
    ).astype(jnp.bfloat16)
    message = layer_norm(
        jnp.dot(hidden_two, w_out, preferred_element_type=jnp.float32) + bias_out, edge_gain
    )
    message = message.reshape(receiver_part.shape[0], fanout, width)
    live = jnp.arange(fanout, dtype=jnp.int32)[None, :] < count_block[:, None]
    return jnp.sum(jnp.where(live[:, :, None], message, 0.0), axis=1)


def layer_core(
    valid_count, own_rows32, sender_rows, w_receive, edge_hid, node_in, node_out, biases, gains
):
    row_count = own_rows32.shape[0]
    width = own_rows32.shape[-1]
    fanout = sender_rows.shape[1]
    own_rows = own_rows32.astype(jnp.bfloat16)
    receiver_term = jnp.dot(
        own_rows, w_receive.astype(jnp.bfloat16), preferred_element_type=jnp.float32
    )
    block_rows = math.gcd(row_count, 256)
    blocks = row_count // block_rows
    w_mid = edge_hid[0].astype(jnp.bfloat16)
    w_out = edge_hid[1].astype(jnp.bfloat16)
    checked = jax.checkpoint(edge_block)

    def one_block(pieces):
        return checked(
            pieces[0], pieces[1], pieces[2], w_mid, w_out, biases[0], biases[1], biases[2], gains[0]
        )

    summed = lax.map(
        one_block,
        (
            receiver_term.reshape(blocks, block_rows, width),
            sender_rows.reshape(blocks, block_rows, fanout, width),
            valid_count.reshape(blocks, block_rows),
        ),
    )
    aggregate = summed.reshape(row_count, width).astype(jnp.bfloat16)
    node_hidden = jax.nn.silu(
        jnp.dot(own_rows, node_in[0].astype(jnp.bfloat16), preferred_element_type=jnp.float32)
        + jnp.dot(aggregate, node_in[1].astype(jnp.bfloat16), preferred_element_type=jnp.float32)
        + biases[3]
    ).astype(jnp.bfloat16)
    update = layer_norm(
        jnp.dot(node_hidden, node_out.astype(jnp.bfloat16), preferred_element_type=jnp.float32)
        + biases[4],
        gains[1],
    )
    return own_rows32 + update


def edge_index_blocks(neighbours):
    row_count = neighbours.shape[0]
    block_rows = math.gcd(row_count, 256)
    return neighbours.reshape(row_count // block_rows, block_rows * neighbours.shape[1])


def gather_neighbours(index_blocks, table_bf):
    rows = lax.map(lambda index: pick_rows(index, table_bf), index_blocks)
    return rows.reshape(-1, table_bf.shape[1])


def scatter_neighbours(index_blocks, grads, table_rows):
    width = grads.shape[1]
    grad_blocks = grads.reshape(index_blocks.shape[0], index_blocks.shape[1], width)

    def add_block(total, pieces):
        return (total + place_rows(pieces[0], pieces[1], table_rows), None)

    total, _ = lax.scan(
        add_block, jnp.zeros((table_rows, width), jnp.float32), (index_blocks, grad_blocks)
    )
    return total


def moved_x(values, shift_by):
    return from_behind(values, "bx", shift_by)


def moved_y(values, shift_by):
    return from_behind(values, "by", shift_by)


def along_x(values, shift_by):
    return from_behind(values, "bx", shift_by)


def along_y(values, shift_by):
    return from_behind(values, "by", shift_by)


def return_x(values, shift_by):
    return from_behind(values.astype(jnp.bfloat16), "bx", shift_by).astype(values.dtype)


def return_y(values, shift_by):
    return from_behind(values.astype(jnp.bfloat16), "by", shift_by).astype(values.dtype)


def route(buffers):
    empty_slot = jnp.zeros_like(buffers[0])
    plus_x = moved_x(buffers[6:9], 1)
    minus_x = moved_x(buffers[0:3], -1)
    plus_y = moved_y(jnp.stack([buffers[5], plus_x[2], minus_x[2]]), 1)
    minus_y = moved_y(jnp.stack([buffers[3], plus_x[0], minus_x[0]]), -1)
    return jnp.stack(
        [
            minus_y[2],
            minus_x[1],
            plus_y[2],
            minus_y[0],
            empty_slot,
            plus_y[0],
            minus_y[1],
            plus_x[1],
            plus_y[1],
        ]
    )


def spread(state, face_lists, corner_lists):
    face_end = face_lists.shape[1]
    corner_end = face_end + corner_lists.shape[1]
    width = state.shape[1]
    face_rows = pick_rows(face_lists.reshape(-1), state).reshape(4, face_end, width)
    corner_rows = pick_rows(corner_lists.reshape(-1), state).reshape(
        4, corner_lists.shape[1], width
    )
    plus_x = along_x(jnp.concatenate([face_rows[0], corner_rows[0], corner_rows[1]]), 1)
    minus_x = along_x(jnp.concatenate([face_rows[1], corner_rows[2], corner_rows[3]]), -1)
    plus_y = along_y(
        jnp.concatenate([face_rows[2], plus_x[face_end:corner_end], minus_x[face_end:corner_end]]),
        1,
    )
    minus_y = along_y(
        jnp.concatenate([face_rows[3], plus_x[corner_end:], minus_x[corner_end:]]), -1
    )
    return jnp.concatenate(
        [
            plus_x[:face_end],
            minus_x[:face_end],
            plus_y[:face_end],
            minus_y[:face_end],
            plus_y[face_end:corner_end],
            minus_y[face_end:corner_end],
            plus_y[corner_end:],
            minus_y[corner_end:],
        ]
    )


def collect(halo_grad, face_lists, corner_lists, row_count):
    face_size = face_lists.shape[1]
    corner_size = corner_lists.shape[1]
    corner_end = face_size + corner_size
    width = halo_grad.shape[1]
    face_part = halo_grad[: 4 * face_size].reshape(4, face_size, width)
    corner_part = halo_grad[4 * face_size :].reshape(4, corner_size, width)
    from_plus_y = return_y(jnp.concatenate([face_part[2], corner_part[0], corner_part[2]]), -1)
    from_minus_y = return_y(jnp.concatenate([face_part[3], corner_part[1], corner_part[3]]), 1)
    from_plus_x = return_x(
        jnp.concatenate(
            [face_part[0], from_plus_y[face_size:corner_end], from_minus_y[face_size:corner_end]]
        ),
        -1,
    )
    from_minus_x = return_x(
        jnp.concatenate([face_part[1], from_plus_y[corner_end:], from_minus_y[corner_end:]]), 1
    )
    targets = jnp.concatenate(
        [
            face_lists[0],
            corner_lists[0],
            corner_lists[1],
            face_lists[1],
            corner_lists[2],
            corner_lists[3],
            face_lists[2],
            face_lists[3],
        ]
    )
    values = jnp.concatenate(
        [from_plus_x, from_minus_x, from_plus_y[:face_size], from_minus_y[:face_size]]
    )
    return place_rows(targets, values, row_count)


def shards(
    latent,
    move_to,
    move_slot,
    arrive_from,
    arrive_slot,
    neighbours,
    valid_count,
    face_send,
    corner_send,
    edge_in,
    edge_hid,
    node_in,
    node_out,
    biases,
    gains,
    grad_out,
):
    row_count = latent.shape[0]
    width = latent.shape[1]
    fanout = neighbours.shape[1]
    face_lists = face_send.reshape(4, -1)
    corner_lists = corner_send.reshape(4, -1)
    slots = CAP
    send_target = jnp.where(move_to == 4, -1, move_to * slots + move_slot)
    outgoing = fill_slots(send_target, latent, 9 * slots).reshape(9, slots, width)
    arrived = route(outgoing)
    pool = jnp.concatenate([arrived.reshape(9 * slots, width), latent])
    picks = jnp.where(arrive_from == 4, 9 * slots + arrive_slot, arrive_from * slots + arrive_slot)
    state = pick_rows(picks, pool)
    weights32 = (
        edge_in.astype(jnp.float32),
        edge_hid.astype(jnp.float32),
        node_in.astype(jnp.float32),
        node_out.astype(jnp.float32),
        biases,
        gains,
    )
    core_fn = partial(layer_core, valid_count)
    index_blocks = edge_index_blocks(neighbours)
    saved = []
    for layer_idx in range(LAYERS):
        halo_rows = spread(state, face_lists, corner_lists)
        table_bf = jnp.concatenate([state, halo_rows])
        gathered = gather_neighbours(index_blocks, table_bf)
        w_send = weights32[0][layer_idx, 1].astype(jnp.bfloat16)
        sender_rows = jnp.dot(gathered, w_send, preferred_element_type=jnp.float32).reshape(
            row_count, fanout, width
        )
        output, pullback = jax.vjp(
            core_fn,
            state.astype(jnp.float32),
            sender_rows,
            weights32[0][layer_idx, 0],
            weights32[1][layer_idx],
            weights32[2][layer_idx],
            weights32[3][layer_idx],
            weights32[4][layer_idx],
            weights32[5][layer_idx],
        )
        saved.append((pullback, gathered, w_send, table_bf.shape[0]))
        state = output.astype(jnp.bfloat16)
    cotangent = grad_out.astype(jnp.float32)
    layer_grads = [None] * LAYERS
    rounded = grad_out
    for layer_idx in reversed(range(LAYERS)):
        pullback, gathered, w_send, table_rows = saved[layer_idx]
        pieces = pullback(cotangent)
        edge_grads = pieces[1].reshape(row_count * fanout, width)
        pair = split_pair(edge_grads)
        both = jnp.einsum("rd,re->de", gathered, pair, preferred_element_type=jnp.float32)
        send_weight_grad = lax.optimization_barrier(
            (both[:, :width] + both[:, width:]).astype(jnp.bfloat16)
        ).astype(jnp.float32)
        sender_grad = scatter_neighbours(index_blocks, edge_grads, table_rows)
        sender_pair = split_pair(sender_grad)
        table_grad = jnp.dot(
            sender_pair[:, :width], w_send.T, preferred_element_type=jnp.float32
        ) + jnp.dot(sender_pair[:, width:], w_send.T, preferred_element_type=jnp.float32)
        table_grad = lax.optimization_barrier(table_grad.astype(jnp.bfloat16)).astype(jnp.float32)
        own_grad = (
            pieces[0]
            + table_grad[:row_count]
            + collect(table_grad[row_count:], face_lists, corner_lists, row_count)
        )
        rounded = own_grad.astype(jnp.bfloat16)
        cotangent = lax.optimization_barrier(rounded).astype(jnp.float32)
        members = (
            jnp.stack([pieces[2], send_weight_grad]),
            pieces[3],
            pieces[4],
            pieces[5],
            pieces[6],
            pieces[7],
        )
        layer_grads[layer_idx] = members
    stacked = [
        jnp.stack([layer_grads[layer_idx][member] for layer_idx in range(LAYERS)])
        for member in range(6)
    ]
    stacked = lax.psum(
        (stacked[0], stacked[1], stacked[2], stacked[3], stacked[4], stacked[5]), ("bx", "by")
    )
    back_target = jnp.where(arrive_from == 4, -1, arrive_from * slots + arrive_slot)
    returning = fill_slots(back_target, rounded, 9 * slots).reshape(9, slots, width)
    returned = jnp.flip(route(jnp.flip(returning, 0)), 0)
    back_pool = jnp.concatenate([returned.reshape(9 * slots, width), rounded])
    back_picks = jnp.where(move_to == 4, 9 * slots + move_slot, move_to * slots + move_slot)
    grad_latent = pick_rows(back_picks, back_pool)
    return (
        state,
        grad_latent,
        stacked[0],
        stacked[1],
        stacked[2],
        stacked[3],
        stacked[4],
        stacked[5],
    )


def solution(mesh):
    placed = (
        P(("bx", "by"), None),
        P(("bx", "by")),
        P(("bx", "by")),
        P(("bx", "by")),
        P(("bx", "by")),
        P(("bx", "by"), None),
        P(("bx", "by")),
        P("bx", "by", None, None),
        P("bx", "by", None, None),
        P(),
        P(),
        P(),
        P(),
        P(),
        P(),
        P(("bx", "by"), None),
    )
    return jax.shard_map(
        shards,
        mesh=mesh,
        in_specs=placed,
        out_specs=(P(("bx", "by"), None), P(("bx", "by"), None), P(), P(), P(), P(), P(), P()),
        check_vma=False,
    )
```

profile of v0, /device:TPU:1, one launch (start us, length us, event | category | flops | bytes accessed | tf_op | source)
XLA Modules:
  0.0 554.4 jit_solution(12585714279460175569)
XLA Ops:
  9.7 7.1 %collective-permute-start.1 = (bf16[3,32,128]{2,1,0:T(8,128)(2,1)S(1)}, bf16[3,32,128]{2,1,0:T(8,128)(2,1)S(1)}, u32[]{:S(2)}, u32[]{:S(2)}) collective-permute-start(bf16[3,32,128]{2,1,0:T(8,128)(2,1)S(1)} %bitcast.598), channel_id=1, source_target_pairs={{0,112},{16,0},{32,16},{48,32},{64,48},{80,64},{96,80},{112,96},{1... | collective-permute-start | bytes 73736 | tf_op jit(solution)/shard_map/ppermute | solution.py:16
  23.1 2.2 collective-permute-start.2
  34.6 5.1 collective-permute-start.5
  41.5 3.2 collective-permute-start.6
  45.6 2.4 collective-permute-done.7
  48.4 8.9 %while.116 = (s32[]{:T(128)}, bf16[2,4096,128]{2,1,0:T(8,128)(2,1)S(1)}, s32[2,4096]{1,0:T(2,128)S(1)}, bf16[832,128]{1,0:T(8,128)(2,1)S(1)}, s32[]{:T(128)}) while((s32[]{:T(128)}, bf16[2,4096,128]{2,1,0:T(8,128)(2,1)S(1)}, s32[2,4096]{1,0:T(2,128)S(1)}, bf16[832,128]{1,0:T(8,128)(2,1)S(1)}, s32[]{:T(128)}) %tuple.345), condition=%wide.region_1.2_spmd, body=%wide.region_0.1_spmd.sunk | while | flops 876347392 | bytes 1310797 | solution.py:119
  48.4 4.4 fusion.394
  52.9 4.4 fusion.394
  57.3 2.7 fusion.190
  60.7 18.4 %while.118 = (s32[]{:T(128)}, bf16[2,256,128]{2,1,0:T(8,128)(2,1)}, s32[2,256]{1,0:T(2,128)S(1)}, f32[2,256,128]{2,1,0:T(8,128)S(1)}, f32[2,256,16,128]{3,2,1,0:...) while((s32[]{:T(128)}, bf16[2,256,128]{2,1,0:T(8,128)(2,1)}, ...), condition=%wide.region_6.7_spmd.clone, body=%wide.region_2.6_spmd.clone.sunk | while | flops 280469504 | bytes 16557421 | solution.py:90
  85.3 6.0 %collective-permute-start.9 = (bf16[96,128]{1,0:T(8,128)(2,1)S(1)}, bf16[96,128]{1,0:T(8,128)(2,1)S(1)}, u32[]{:S(2)}, u32[]{:S(2)}) collective-permute-start(bf16[96,128]{1,0:T(8,128)(2,1)S(1)} %pad_maximum_fusion.9), channel_id=1, source_target_pairs={{0,112},{16,0},{32,16},{48,32},{64,48},{80,64},{96,80},{112,96},{1... | collective-permute-start | bytes 73736 | tf_op jit(solution)/shard_map/ppermute | solution.py:16
  96.3 8.9 %while.117 = (s32[]{:T(128)}, bf16[2,4096,128]{2,1,0:T(8,128)(2,1)S(1)}, s32[2,4096]{1,0:T(2,128)S(1)}, bf16[832,128]{1,0:T(8,128)(2,1)S(1)}, s32[]{:T(128)}) while((s32[]{:T(128)}, bf16[2,4096,128]{2,1,0:T(8,128)(2,1)S(1)}, s32[2,4096]{1,0:T(2,128)S(1)}, bf16[832,128]{1,0:T(8,128)(2,1)S(1)}, s32[]{:T(128)}) %tuple.380), condition=%wide.region_10.11_spmd, body=%wide.region_9.10_spmd.sunk | while | flops 876347392 | bytes 1310797 | solution.py:119
  96.4 4.4 fusion.396
  100.8 4.4 fusion.396
  105.3 2.7 fusion.186
  108.1 16.9 %while.119 = (s32[]{:T(128)}, bf16[2,256,128]{2,1,0:T(8,128)(2,1)S(1)}, s32[2,256]{1,0:T(2,128)S(1)}, f32[2,256,128]{2,1,0:T(8,128)}, f32[2,256,16,128]{3,2,1,0:...) while((s32[]{:T(128)}, ...), condition=%wide.region_15.16_spmd.clone, body=%wide.region_11.15_spmd.clone.sunk | while | flops 280469504 | bytes 15496333 | solution.py:90
  134.5 2.3 broadcast.603.clone
  136.8 47.8 %while.120 = (s32[]{:T(128)}, f32[5,128]{1,0:T(8,128)S(1)}, f32[2,128]{1,0:T(2,128)}, bf16[128,128]{1,0:T(8,128)(2,1)}, bf16[128,128]{1,0:T(8,128)(2,1)}, /*inde...) while((s32[]{:T(128)}, f32[5,128]{1,0:T(8,128)S(1)}, ...), condition=%wide.region_30.31_spmd.clone, body=%wide.region_20.30_spmd.clone.sunk | while | flops 841566720 | bytes 123291448 | solution.py:90
  140.9 2.5 convolution_add_fusion.16
  146.8 2.5 fusion.414
  164.5 2.5 convolution_add_fusion.16
  170.5 2.5 fusion.414
  187.5 13.3 %while.121 = (s32[]{:T(128)}, f32[832,128]{1,0:T(8,128)}, s32[2,4096]{1,0:T(2,128)}, f32[2,4096,128]{2,1,0:T(8,128)}, s32[]{:T(128)}, /*index=5*/s32[]{:T(128)}) while((s32[]{:T(128)}, f32[832,128]{1,0:T(8,128)}, s32[2,4096]{1,0:T(2,128)}, f32[2,4096,128]{2,1,0:T(8,128)}, s32[]{:T(128)}, /*index=5*/s32[]{:T(128)}) %tuple.381), condition=%wide.region_32.33_spmd.clone, body=%wide.region_31.32_spmd.clone.sunk | while | flops 1754324992 | bytes 13353111 | solution.py:130
  188.3 2.5 fusion.424
  190.8 2.2 fusion.425
  194.8 2.5 fusion.424
  197.3 2.2 fusion.425
  203.4 2.9 fusion.86
  206.2 2.8 collective-permute-start.12
  210.7 4.4 collective-permute-done.13
  216.3 4.3 collective-permute-start.14
  228.7 2.3 broadcast.603
  231.0 44.7 %while.122 = (s32[]{:T(128)}, f32[5,128]{1,0:T(8,128)S(1)}, f32[2,128]{1,0:T(2,128)S(1)}, bf16[128,128]{1,0:T(8,128)(2,1)S(1)}, bf16[128,128]{1,0:T(8,128)(2,1)}...) while((s32[]{:T(128)}, f32[5,128]{1,0:T(8,128)S(1)}, ...), condition=%wide.region_45.46_spmd.clone, body=%wide.region_35.45_spmd.clone.sunk | while | flops 841566720 | bytes 122754632 | solution.py:90
  239.8 2.5 fusion.436
  262.2 2.5 fusion.436
  278.1 11.8 %while.123 = (s32[]{:T(128)}, f32[832,128]{1,0:T(8,128)}, s32[2,4096]{1,0:T(2,128)S(1)}, f32[2,4096,128]{2,1,0:T(8,128)}, s32[]{:T(128)}, /*index=5*/s32[]{:T(128)}) while((s32[]{:T(128)}, f32[832,128]{1,0:T(8,128)}, s32[2,4096]{1,0:T(2,128)S(1)}, f32[2,4096,128]{2,1,0:T(8,128)}, s32[]{:T(128)}, /*index=5*/s32[]{:T(128)}) %tuple.382), condition=%wide.region_47.48_spmd.clone, body=%wide.region_46.47_spmd.clone.sunk | while | flops 1754324992 | bytes 13353111 | solution.py:130
  278.1 2.5 fusion.446
  280.7 2.2 fusion.447
  284.0 2.5 fusion.446
  286.5 2.2 fusion.447
  292.7 2.9 fusion.87
  295.5 5.6 %collective-permute-start.16 = (bf16[96,128]{1,0:T(8,128)(2,1)S(1)}, bf16[96,128]{1,0:T(8,128)(2,1)S(1)}, u32[]{:S(2)}, u32[]{:S(2)}) collective-permute-start(bf16[96,128]{1,0:T(8,128)(2,1)S(1)} %pad_maximum_fusion.16), channel_id=1, source_target_pairs={{0,15},{1,0},{2,1},{3,2},{4,3},{5,4},{6,5},{7,6},{8,7},{9,8},{10,9... | collective-permute-start | bytes 73736 | tf_op jit(solution)/shard_map/ppermute | solution.py:16
  306.0 4.4 collective-permute-start.18
  313.1 5.2 collective-permute-start.21
  319.3 5.3 collective-permute-done.20
  324.6 4.5 collective-permute-start.22
  330.0 64.3 %all-reduce.22 = (f32[2,5,128]{2,1,0:T(8,128)S(1)}, f32[2,2,128]{2,1,0:T(2,128)}) all-reduce(f32[2,5,128]{2,1,0:T(8,128)S(1)} %pad_maximum_fusion.22, f32[2,2,128]{2,1,0:T(2,128)S(1)} %pad_maximum_fusion.23), channel_id=1, replica_groups=mesh['bx'=8,'by'=16] {'bx','by'}, use_global_device_ids=true, to_apply=%region_56.57 | all-reduce | flops 1792 | bytes 14336 | tf_op jit(solution)/shard_map/psum | solution.py:348
  396.2 144.4 %all-reduce.26.cloned.1.call-done = (f32[2,2,128,128]{3,2,1,0:T(8,128)}, f32[2,2,128,128]{3,2,1,0:T(8,128)}, f32[2,2,128,128]{3,2,1,0:T(8,128)}, f32[2,128,128]{2,1,0:T(8,128)}) async-done(((f32[2,2,128,128]{3,2,1,0:T(8,128)}, f32[2,2,128,128]{3,2,1,0:T(8,128)}, f32[2,2,128,128]{3,2,1,0:T(8,128)}, f32[2,128,128]{2,1,0:T(8,128)}), (f32[2,2,128,128]{3,2,1,0:T(8,128)}, f32[2,2,128,128]{3,2,1,0:T(8,128)}, ...) | async-done | bytes 917520 | tf_op jit(solution)/shard_map/psum | solution.py:348
  (743 shorter events, 197.2 us)
Async XLA Ops:
  7.2 533.4 %all-reduce.26.cloned.1.call-start = ((), (), s32[]{:S(2)}) async-start(), calls=%async_computation | async-start | bytes 1835008 | tf_op jit(solution)/shard_map/psum | solution.py:348
  8.5 32.8 %copy-start.55 = (bf16[2,2,128,128]{3,2,1,0:T(8,128)(2,1)S(1)}, bf16[2,2,128,128]{3,2,1,0:T(8,128)(2,1)}, u32[]{:S(2)}) copy-start(bf16[2,2,128,128]{3,2,1,0:T(8,128)(2,1)} %param.41) | copy-start | bytes 393220
  9.7 12.1 %collective-permute-start.1 = (bf16[3,32,128]{2,1,0:T(8,128)(2,1)S(1)}, bf16[3,32,128]{2,1,0:T(8,128)(2,1)S(1)}, u32[]{:S(2)}, u32[]{:S(2)}) collective-permute-start(bf16[3,32,128]{2,1,0:T(8,128)(2,1)S(1)} %bitcast.598), channel_id=1, source_target_pairs={{0,112},{16,0},{32,16},{48,32},{64,48},{80,64},{96,80},{112,96},{1... | collective-permute-start | bytes 73736 | tf_op jit(solution)/shard_map/ppermute | solution.py:16
  16.8 6.3 %collective-permute-start = (bf16[3,32,128]{2,1,0:T(8,128)(2,1)S(1)}, bf16[3,32,128]{2,1,0:T(8,128)(2,1)S(1)}, u32[]{:S(2)}, u32[]{:S(2)}) collective-permute-start(bf16[3,32,128]{2,1,0:T(8,128)(2,1)S(1)} %bitcast.597), channel_id=1, source_target_pairs={{0,16},{16,32},{32,48},{48,64},{64,80},{80,96},{96,112},{112,0},{1... | collective-permute-start | bytes 73736 | tf_op jit(solution)/shard_map/ppermute | solution.py:16
  23.1 3.9 collective-permute-start.2
  27.0 5.4 collective-permute-start.3
  30.0 18.4 %copy-start.116 = (s32[256]{0:T(256)}, s32[256]{0:T(256)S(1)}, u32[]{:S(2)}) copy-start(s32[256]{0:T(256)S(1)} %eq.118) | copy-start | bytes 3076
  33.9 14.4 %copy-start.27 = (bf16[512,128]{1,0:T(8,128)(2,1)}, bf16[512,128]{1,0:T(8,128)(2,1)S(1)}, u32[]{:S(2)}) copy-start(bf16[512,128]{1,0:T(8,128)(2,1)S(1)} %get-tuple-element.1648) | copy-start | bytes 393220
  34.5 7.0 %collective-permute-start.4 = (bf16[96,128]{1,0:T(8,128)(2,1)S(1)}, bf16[96,128]{1,0:T(8,128)(2,1)S(1)}, u32[]{:S(2)}, u32[]{:S(2)}) collective-permute-start(bf16[96,128]{1,0:T(8,128)(2,1)S(1)} %pad_maximum_fusion.4), channel_id=1, source_target_pairs={{0,16},{16,32},{32,48},{48,64},{64,80},{80,96},{96,112},{112,0},{1... | collective-permute-start | bytes 73736 | tf_op jit(solution)/shard_map/ppermute | solution.py:16
  34.6 6.9 %collective-permute-start.5 = (bf16[96,128]{1,0:T(8,128)(2,1)S(1)}, bf16[96,128]{1,0:T(8,128)(2,1)S(1)}, u32[]{:S(2)}, u32[]{:S(2)}) collective-permute-start(bf16[96,128]{1,0:T(8,128)(2,1)S(1)} %pad_maximum_fusion.5), channel_id=1, source_target_pairs={{0,112},{16,0},{32,16},{48,32},{64,48},{80,64},{96,80},{112,96},{1... | collective-permute-start | bytes 73736 | tf_op jit(solution)/shard_map/ppermute | solution.py:16
  41.5 4.1 collective-permute-start.6
  44.7 3.4 collective-permute-start.7
  60.7 18.5 %copy-start.111 = (f32[128]{0:T(128)S(1)}, f32[128]{0:T(128)}, u32[]{:S(2)}) copy-start(f32[128]{0:T(128)} %get-tuple-element.1623) | copy-start | bytes 1540
  60.7 19.9 %copy-start.127 = (f32[128]{0:T(128)S(1)}, f32[128]{0:T(128)}, u32[]{:S(2)}) copy-start(f32[128]{0:T(128)} %get-tuple-element.1622) | copy-start | bytes 1540
  79.1 13.1 %copy-start.14 = (f32[2,256,128]{2,1,0:T(8,128)}, f32[2,256,128]{2,1,0:T(8,128)S(1)}, u32[]{:S(2)}) copy-start(f32[2,256,128]{2,1,0:T(8,128)S(1)} %get-tuple-element.2499) | copy-start | bytes 786436
  80.6 15.8 %copy-start.60 = (f32[512,128]{1,0:T(8,128)}, f32[512,128]{1,0:T(8,128)S(1)}, u32[]{:S(2)}) copy-start(f32[512,128]{1,0:T(8,128)S(1)} %fusion.93) | copy-start | bytes 786436
  81.7 14.3 %copy-start.19 = (f32[512,128]{1,0:T(8,128)}, f32[512,128]{1,0:T(8,128)S(1)}, u32[]{:S(2)}) copy-start(f32[512,128]{1,0:T(8,128)S(1)} %get-tuple-element.1650) | copy-start | bytes 786436
  81.7 14.6 %copy-start.74 = (f32[512]{0:T(512)}, f32[512]{0:T(512)S(1)}, u32[]{:S(2)}) copy-start(f32[512]{0:T(512)S(1)} %broadcast_multiply_fusion.5) | copy-start | bytes 6148
  82.7 13.6 %copy-start.25 = (s32[2,4096]{1,0:T(2,128)S(1)}, s32[2,4096]{1,0:T(2,128)}, u32[]{:S(2)}) copy-start(s32[2,4096]{1,0:T(2,128)} %copy-done.24) | copy-start | bytes 98308
  85.2 7.4 %collective-permute-start.8 = (bf16[96,128]{1,0:T(8,128)(2,1)S(1)}, bf16[96,128]{1,0:T(8,128)(2,1)S(1)}, u32[]{:S(2)}, u32[]{:S(2)}) collective-permute-start(bf16[96,128]{1,0:T(8,128)(2,1)S(1)} %pad_maximum_fusion.8), channel_id=1, source_target_pairs={{0,16},{16,32},{32,48},{48,64},{64,80},{80,96},{96,112},{112,0},{1... | collective-permute-start | bytes 73736 | tf_op jit(solution)/shard_map/ppermute | solution.py:16
  85.3 7.3 %collective-permute-start.9 = (bf16[96,128]{1,0:T(8,128)(2,1)S(1)}, bf16[96,128]{1,0:T(8,128)(2,1)S(1)}, u32[]{:S(2)}, u32[]{:S(2)}) collective-permute-start(bf16[96,128]{1,0:T(8,128)(2,1)S(1)} %pad_maximum_fusion.9), channel_id=1, source_target_pairs={{0,112},{16,0},{32,16},{48,32},{64,48},{80,64},{96,80},{112,96},{1... | collective-permute-start | bytes 73736 | tf_op jit(solution)/shard_map/ppermute | solution.py:16
  92.6 1.4 collective-permute-start.10
  92.7 3.3 collective-permute-start.11
  108.0 16.9 %copy-start.110 = (f32[128]{0:T(128)S(1)}, f32[128]{0:T(128)}, u32[]{:S(2)}) copy-start(f32[128]{0:T(128)} %get-tuple-element.1628) | copy-start | bytes 1540
  108.1 18.1 %copy-start.124 = (f32[128]{0:T(128)S(1)}, f32[128]{0:T(128)}, u32[]{:S(2)}) copy-start(f32[128]{0:T(128)} %get-tuple-element.1627) | copy-start | bytes 1540
  187.4 13.3 %copy-start.57 = (bf16[2,2,128,128]{3,2,1,0:T(8,128)(2,1)S(1)}, bf16[2,2,128,128]{3,2,1,0:T(8,128)(2,1)}, u32[]{:S(2)}) copy-start(bf16[2,2,128,128]{3,2,1,0:T(8,128)(2,1)} %param.41) | copy-start | bytes 393220
  206.2 4.4 collective-permute-start.12
  209.1 12.7 %copy-start.112 = (s32[320]{0:T(512)S(1)}, s32[320]{0:T(512)}, u32[]{:S(2)}) copy-start(s32[320]{0:T(512)} %concatenate.117) | copy-start | bytes 3844
  209.1 13.0 %copy-start.37 = (bf16[512,128]{1,0:T(8,128)(2,1)S(1)}, bf16[512,128]{1,0:T(8,128)(2,1)}, u32[]{:S(2)}) copy-start(bf16[512,128]{1,0:T(8,128)(2,1)} %copy-done.36) | copy-start | bytes 393220
  209.1 13.0 %copy-start.49 = (bf16[512,128]{1,0:T(8,128)(2,1)S(1)}, bf16[512,128]{1,0:T(8,128)(2,1)}, u32[]{:S(2)}) copy-start(bf16[512,128]{1,0:T(8,128)(2,1)} %param.47) | copy-start | bytes 393220
  209.1 13.0 %copy-start.59 = (bf16[2,2,128,128]{3,2,1,0:T(8,128)(2,1)S(1)}, bf16[2,2,128,128]{3,2,1,0:T(8,128)(2,1)}, u32[]{:S(2)}) copy-start(bf16[2,2,128,128]{3,2,1,0:T(8,128)(2,1)} %param.43) | copy-start | bytes 393220
  210.0 12.4 %copy-start.20 = (f32[512,128]{1,0:T(8,128)S(1)}, f32[512,128]{1,0:T(8,128)}, u32[]{:S(2)}) copy-start(f32[512,128]{1,0:T(8,128)} %copy-done.19) | copy-start | bytes 786436
  210.0 12.4 %copy-start.75 = (f32[512]{0:T(512)S(1)}, f32[512]{0:T(512)}, u32[]{:S(2)}) copy-start(f32[512]{0:T(512)} %copy-done.74) | copy-start | bytes 6148
  210.0 13.1 %copy-start.96 = (f32[512]{0:T(512)S(1)}, f32[512]{0:T(512)}, u32[]{:S(2)}) copy-start(f32[512]{0:T(512)} %copy-done.95) | copy-start | bytes 6148
  210.6 13.6 %copy-start.61 = (f32[512,128]{1,0:T(8,128)S(1)}, f32[512,128]{1,0:T(8,128)}, u32[]{:S(2)}) copy-start(f32[512,128]{1,0:T(8,128)} %copy-done.60) | copy-start | bytes 786436
  210.6 4.4 collective-permute-start.13
  215.1 6.7 %collective-permute-start.15 = (bf16[96,128]{1,0:T(8,128)(2,1)S(1)}, bf16[96,128]{1,0:T(8,128)(2,1)S(1)}, u32[]{:S(2)}, u32[]{:S(2)}) collective-permute-start(bf16[96,128]{1,0:T(8,128)(2,1)S(1)} %pad_maximum_fusion.15), channel_id=1, source_target_pairs={{0,16},{16,32},{32,48},{48,64},{64,80},{80,96},{96,112},{112,0},{1... | collective-permute-start | bytes 73736 | tf_op jit(solution)/shard_map/ppermute | solution.py:16
  216.3 5.5 collective-permute-start.14
  231.0 47.0 %copy-start.26 = (s32[2,4096]{1,0:T(2,128)S(1)}, s32[2,4096]{1,0:T(2,128)}, u32[]{:S(2)}) copy-start(s32[2,4096]{1,0:T(2,128)} %get-tuple-element.2504) | copy-start | bytes 98308
  295.5 9.1 %collective-permute-start.16 = (bf16[96,128]{1,0:T(8,128)(2,1)S(1)}, bf16[96,128]{1,0:T(8,128)(2,1)S(1)}, u32[]{:S(2)}, u32[]{:S(2)}) collective-permute-start(bf16[96,128]{1,0:T(8,128)(2,1)S(1)} %pad_maximum_fusion.16), channel_id=1, source_target_pairs={{0,15},{1,0},{2,1},{3,2},{4,3},{5,4},{6,5},{7,6},{8,7},{9,8},{10,9... | collective-permute-start | bytes 73736 | tf_op jit(solution)/shard_map/ppermute | solution.py:16
  301.2 3.5 collective-permute-start.17
  304.7 6.7 %collective-permute-start.19 = (bf16[96,128]{1,0:T(8,128)(2,1)S(1)}, bf16[96,128]{1,0:T(8,128)(2,1)S(1)}, u32[]{:S(2)}, u32[]{:S(2)}) collective-permute-start(bf16[96,128]{1,0:T(8,128)(2,1)S(1)} %pad_maximum_fusion.19), channel_id=1, source_target_pairs={{0,16},{16,32},{32,48},{48,64},{64,80},{80,96},{96,112},{112,0},{1... | collective-permute-start | bytes 73736 | tf_op jit(solution)/shard_map/ppermute | solution.py:16
  306.0 5.5 collective-permute-start.18
  311.0 84.1 %copy-start.114 = (s32[512]{0:T(512)S(1)}, s32[512]{0:T(512)}, u32[]{:S(2)}) copy-start(s32[512]{0:T(512)} %get-tuple-element.1631) | copy-start | bytes 6148
  313.1 6.2 %collective-permute-start.21 = (bf16[3,32,128]{2,1,0:T(8,128)(2,1)S(1)}, bf16[3,32,128]{2,1,0:T(8,128)(2,1)S(1)}, u32[]{:S(2)}, u32[]{:S(2)}) collective-permute-start(bf16[3,32,128]{2,1,0:T(8,128)(2,1)S(1)} %slice.802), channel_id=1, source_target_pairs={{0,112},{16,0},{32,16},{48,32},{64,48},{80,64},{96,80},{112,96},{1... | collective-permute-start | bytes 73736 | tf_op jit(solution)/shard_map/ppermute | solution.py:16
  318.3 6.3 %collective-permute-start.20 = (bf16[3,32,128]{2,1,0:T(8,128)(2,1)S(1)}, bf16[3,32,128]{2,1,0:T(8,128)(2,1)S(1)}, u32[]{:S(2)}, u32[]{:S(2)}) collective-permute-start(bf16[3,32,128]{2,1,0:T(8,128)(2,1)S(1)} %slice.798), channel_id=1, source_target_pairs={{0,16},{16,32},{32,48},{48,64},{64,80},{80,96},{96,112},{112,0},{1... | collective-permute-start | bytes 73736 | tf_op jit(solution)/shard_map/ppermute | solution.py:16
  324.6 5.3 collective-permute-start.22
  329.9 65.0 %collective-permute-start.23 = (bf16[3,32,128]{2,1,0:T(8,128)(2,1)S(1)}, bf16[3,32,128]{2,1,0:T(8,128)(2,1)S(1)}, u32[]{:S(2)}, u32[]{:S(2)}) collective-permute-start(bf16[3,32,128]{2,1,0:T(8,128)(2,1)S(1)} %pad_maximum_fusion.21), channel_id=1, source_target_pairs={{0,1},{1,2},{2,3},{3,4},{4,5},{5,6},{6,7},{7,8},{8,9},{9,10},{10,1... | collective-permute-start | bytes 73736 | tf_op jit(solution)/shard_map/ppermute | solution.py:16
  (155 other events, 430.8 us)
Sparse Core Ops, SparseCore 0:
  395.1 145.5 all-reduce.25
where the time goes:
time: 566 us; the launch traced here: 554 us
  waiting for transfers between devices  165 us (29%)
  matrix products  105 us (19%)
  local copies, waits for them, and re-layouts  83.9 us (15%)
  blocking collectives  64.3 us (11%)
  other arithmetic  63.2 us (11%)
  starting transfers between devices  53.9 us (10%)
  between operations  16.2 us (3%)
    psum x1, waiting for transfers between devices, shards(): lax.psum((stacked[0], stacked[1], stacked[2], stacked[3], stacked[4], sta...  144 us
    psum x1, blocking collectives, shards(): lax.psum((stacked[0], stacked[1], stacked[2], stacked[3], stacked[4], sta...  64.3 us
    ppermute x24, starting transfers between devices, from_behind(): return lax.ppermute(value, axis, pairs)  53.9 us
    dot_general x16, matrix products, edge_block(): jnp.dot(hidden_two, w_out, preferred_element_type=jnp.float32) + bias_out  24.9 us
    while x176, local copies, waits for them, and re-layouts  22.4 us
    dot_general x10, matrix products, pick_rows(): jnp.dot(hits, source, preferred_element_type=jnp.float32)  21.1 us
    ppermute x24, waiting for transfers between devices, from_behind(): return lax.ppermute(value, axis, pairs)  20.9 us
    convert_element_type x8, other arithmetic, split_pair(): low = (values - high.astype(jnp.float32)).astype(jnp.bfloat16)  15.9 us
  transfers between devices with their start and end apart: 25, of which 14 were waited for; matrix products, arithmetic and copies ran while one was open for 4% of the time, Pallas kernels for 0%

commit v1 on v0

v1 whole, which is shorter than its diff:
```python
import functools

import jax
import jax.numpy as jnp
from jax import lax
from jax.experimental import pallas as pl
from jax.experimental.pallas import tpu as pltpu
from jax.sharding import PartitionSpec as P

LAYERS = 2
CAP = 32
D = 128
K = 16
PAIRS = K // 2
ROWS = 512
HALF = 416
HALO = 320
CODES = 9
SLOTS = CODES * CAP
POOL = 384
GRAD_ROWS = 1024
BLOCK = 256
F32 = jnp.float32
BF16 = jnp.bfloat16
MESH = pl.DeviceIdType.MESH
TRAVEL = tuple((code // 3 - 1, code % 3 - 1) for code in range(CODES))
HALO_BLOCKS = (
    (1, 0, 0, 64),
    (-1, 0, 64, 64),
    (0, 1, 128, 64),
    (0, -1, 192, 64),
    (1, 1, 256, 16),
    (1, -1, 272, 16),
    (-1, 1, 288, 16),
    (-1, -1, 304, 16),
)


def dot(a, b):
    return jnp.dot(a, b, preferred_element_type=F32)


def dot_nt(a, b):
    return lax.dot_general(a, b, (((1,), (1,)), ((), ())), preferred_element_type=F32)


def dot_tn(a, b):
    return lax.dot_general(a, b, (((0,), (0,)), ((), ())), preferred_element_type=F32)


def column(row):
    return jnp.transpose(jnp.broadcast_to(row, (D, row.shape[1])))


def one_hot_lanes(filled, width):
    lane = lax.broadcasted_iota(jnp.int32, filled.shape, 1).astype(F32)
    pieces = [
        jnp.where(filled == lane + float(start), 1.0, 0.0).astype(BF16) for start in range(0, width, D)
    ]
    return jnp.concatenate(pieces, axis=1)


def one_hot_rows(row, height):
    index = lax.broadcasted_iota(jnp.int32, (height, row.shape[1]), 0).astype(F32)
    return jnp.where(index == row, 1.0, 0.0).astype(BF16)


def twice(values):
    return jnp.concatenate([values, values], axis=1)


def partial_sums(values):
    return jnp.sum(values.reshape(values.shape[0] // 8, 8, values.shape[1]), axis=0)


def layer_norm_parts(values):
    centred = values - jnp.mean(values, axis=1, keepdims=True)
    scale = lax.rsqrt(jnp.mean(centred * centred, axis=1, keepdims=True) + 1e-05)
    return centred * scale, scale


def half_silu(half):
    wave = jnp.tanh(half)
    gate = 1.0 + wave
    value = half * gate
    return value, gate + value * (1.0 - wave)


def kernel(
    nx, ny,
    lat, move_to, move_slot, arrive_from, arrive_slot, nbr, count, face, corner,
    e_in, e_hid, n_in, n_out, bia, gai, gout,
    state_o, glat_o, gein_o, gehid_o, gnin_o, gnout_o, gbia_o, ggai_o,
    outgoing, arrived, halo_out, halo_in, ret_out, ret_in, back_out, back_in,
    pick_send, pick_back, hits, hits_t, upper, count_col,
    state, recv_term, send_tab, w_mid, w_out, w_mid_t, w_out_t, ones,
    h1s, h2s, d1s, d2s, xhs, rss, acc, agg, nhs, d3s, xh2s, rs2s,
    dxc, g_rows, g_recv, agg_raw, dsend, dw_out, dw_mid, db_out, db_mid,
    terms, rs_in, ar_buf, final,
    mig_s, mig_r, halo_s, halo_r, ret_s, ret_r, back_s, back_r,
    rs_s, rs_r, ar_s, ar_r, ag_s, ag_r,
):
    a = lax.axis_index("bx")
    b = lax.axis_index("by")
    chunk = GRAD_ROWS // ny

    def at(move_x, move_y):
        return (lax.rem(a + (move_x + nx), nx), lax.rem(b + (move_y + ny), ny))

    def remote(src, dst, send, recv, target):
        return pltpu.make_async_remote_copy(
            src_ref=src, dst_ref=dst, send_sem=send, recv_sem=recv, device_id=target, device_id_type=MESH
        )

    barrier = pltpu.get_barrier_semaphore()
    partners = [(0, step) for step in range(1, ny)] + [(step, 0) for step in range(1, nx)]
    partners += [(1, 1), (1, -1), (-1, 1), (-1, -1)]
    for move_x, move_y in partners:
        pl.semaphore_signal(barrier, inc=1, device_id=at(move_x, move_y), device_id_type=MESH)

    def as_row(ref):
        return ref[...].astype(F32)

    to_row, slot_row = as_row(move_to), as_row(move_slot)
    from_row, aslot_row = as_row(arrive_from), as_row(arrive_slot)
    out_target = jnp.where(to_row == 4.0, -1.0, to_row * CAP + slot_row)
    outgoing[...] = dot(one_hot_rows(out_target, SLOTS), lat[...]).astype(BF16)
    arrived[CAP * 4 : CAP * 5, :] = jnp.zeros((CAP, D), BF16)
    arrived[SLOTS:, :] = jnp.zeros((POOL - SLOTS, D), BF16)
    back_in[CAP * 4 : CAP * 5, :] = jnp.zeros((CAP, D), BF16)
    back_in[SLOTS:, :] = jnp.zeros((POOL - SLOTS, D), BF16)
    pl.semaphore_wait(barrier, len(partners))

    def swap_slots(source, target, send, recv, sign):
        copies = []
        for code, (move_x, move_y) in enumerate(TRAVEL):
            if code == 4:
                continue
            rows = pl.ds(code * CAP, CAP)
            copies.append(
                remote(
                    source.at[rows], target.at[rows], send.at[code], recv.at[code],
                    at(sign * move_x, sign * move_y),
                )
            )
        for copy in copies:
            copy.start()
        return copies

    def swap_halo(source, target, send, recv, sign):
        copies = []
        for index, (move_x, move_y, first, size) in enumerate(HALO_BLOCKS):
            rows = pl.ds(first, size)
            copies.append(
                remote(
                    source.at[rows], target.at[rows], send.at[index], recv.at[index],
                    at(sign * move_x, sign * move_y),
                )
            )
        for copy in copies:
            copy.start()
        return copies

    def landed(copies):
        for copy in copies:
            copy.wait_recv()

    everything = []
    migration = swap_slots(outgoing, arrived, mig_s, mig_r, 1)
    everything += migration

    stay_pick = one_hot_lanes(column(jnp.where(from_row == 4.0, aslot_row, -1.0)), ROWS)
    come_pick = one_hot_lanes(column(jnp.where(from_row == 4.0, -1.0, from_row * CAP + aslot_row)), POOL)
    staying = dot(stay_pick, lat[...])
    for index in range(4):
        filled = column(face[index : index + 1, :].astype(F32))
        pick_send[index * 64 : index * 64 + 64, :] = one_hot_lanes(filled, ROWS)
    for index in range(4):
        filled = column(corner[index : index + 1, :].astype(F32))
        pick_send[256 + index * 16 : 272 + index * 16, :] = one_hot_lanes(filled, ROWS)
    pick_back[...] = jnp.transpose(pick_send[...].astype(F32)).astype(BF16)
    count_col[...] = column(as_row(count))

    def build_hits(k, carry):
        row = nbr[pl.ds(k, 1), :].astype(F32)
        high = row >= float(HALF)
        inner = jnp.where(high, row - float(HALF), row)
        hits[k] = one_hot_lanes(column(inner), ROWS)
        upper[k] = column(jnp.where(high, 1.0, 0.0))
        hits_t[k] = one_hot_rows(inner, HALF)
        return carry

    lax.fori_loop(0, K, build_hits, 0)

    diag = (lax.broadcasted_iota(jnp.int32, (2 * D, 2 * D), 0) // D) == (
        lax.broadcasted_iota(jnp.int32, (2 * D, 2 * D), 1) // D
    )
    ones[...] = jnp.where(diag, 1.0 / D, 0.0).astype(BF16)

    def doubled(weight):
        both = jnp.concatenate([twice(weight), twice(weight)], axis=0)
        return jnp.where(diag, both, 0.0).astype(BF16)

    for layer in range(LAYERS):
        mid = e_hid[layer, 0].astype(F32) * 0.5
        out = e_hid[layer, 1].astype(F32)
        w_mid[layer] = doubled(mid)
        w_mid_t[layer] = doubled(jnp.transpose(mid))
        w_out[layer] = doubled(out - jnp.mean(out, axis=1, keepdims=True))
        w_out_t[layer] = doubled(jnp.transpose(out) * 0.5)
    send_tab[HALF:, :] = jnp.zeros((ROWS - HALF, 2 * D), BF16)

    def bias(layer, index):
        return bia[index, layer : layer + 1, :]

    def gain(layer, index):
        return gai[layer, index : index + 1, :]

    landed(migration)
    state[0] = (staying + dot(come_pick, arrived[...])).astype(BF16)

    def forward(layer):
        halo_out[layer] = dot(pick_send[...], state[layer]).astype(BF16)
        halo = swap_halo(halo_out.at[layer], halo_in.at[layer], halo_s.at[layer], halo_r.at[layer], 1)
        everything.extend(halo)
        own = state[layer]
        recv_term[...] = (dot(own, e_in[layer, 0]) + bias(layer, 0)) * 0.5
        w_send = (e_in[layer, 1].astype(F32) * 0.5).astype(BF16)
        own_send = dot(own, w_send).astype(BF16)
        send_tab[0:HALF, 0:D] = own_send[0:HALF]
        send_tab[0 : ROWS - HALF, D:] = own_send[HALF:]
        acc[...] = jnp.zeros((ROWS, D), F32)
        bias_mid = twice(bias(layer, 1)) * 0.5
        bias_out = bias(layer, 2)
        bias_out = twice(bias_out - jnp.mean(bias_out, axis=1, keepdims=True))
        landed(halo)
        send_tab[ROWS - HALF : HALF, D:] = dot(halo_in[layer], w_send).astype(BF16)

        def pair(j, carry):
            low_slot = j.astype(F32)
            for first in range(0, ROWS, BLOCK):
                rows = slice(first, first + BLOCK)
                parts = []
                for k in (j, j + PAIRS):
                    both = dot(hits[k, rows], send_tab[...])
                    parts.append(recv_term[rows] + jnp.where(upper[k, rows] > 0.5, both[:, D:], both[:, :D]))
                value, slope = half_silu(jnp.concatenate(parts, axis=1))
                value = value.astype(BF16)
                h1s[layer, j, rows] = value
                d1s[layer, j, rows] = slope.astype(BF16)
                value, slope = half_silu(dot(value, w_mid[layer]) + bias_mid)
                value = value.astype(BF16)
                h2s[layer, j, rows] = value
                d2s[layer, j, rows] = slope.astype(BF16)
                centred = dot(value, w_out[layer]) + bias_out
                variance = dot((centred * centred).astype(BF16), ones[...])
                scale = lax.rsqrt(variance + 1e-05)
                live = count_col[rows]
                mask = jnp.concatenate([live > low_slot, live > low_slot + PAIRS], axis=1)
                scale = jnp.where(mask, scale, 0.0)
                normed = centred * scale
                rss[layer, j, rows] = scale.astype(BF16)
                xhs[layer, j, rows] = normed.astype(BF16)
                acc[rows] += normed[:, :D] + normed[:, D:]
            return carry

        lax.fori_loop(0, PAIRS, pair, 0)
        total = acc[...]
        agg_raw[layer] = total
        total = (total * gain(layer, 0)).astype(BF16)
        agg[layer] = total
        half = (dot(own, n_in[layer, 0]) + dot(total, n_in[layer, 1]) + bias(layer, 3)) * 0.5
        value, slope = half_silu(half)
        value = value.astype(BF16)
        nhs[layer] = value
        d3s[layer] = slope
        normed, scale = layer_norm_parts(dot(value, n_out[layer]) + bias(layer, 4))
        xh2s[layer] = normed
        rs2s[layer] = jnp.broadcast_to(scale, (ROWS, D))
        return (own.astype(F32) + normed * gain(layer, 1)).astype(BF16)

    for layer in range(LAYERS):
        following = forward(layer)
        if layer + 1 < LAYERS:
            state[layer + 1] = following
        else:
            state_o[...] = following

    def put_term(layer, index, values):
        terms[layer, index * D : index * D + D, :] = values.astype(BF16)

    def put_rows(layer, rows):
        terms[layer, 7 * D :, :] = jnp.zeros((D, D), BF16)
        stacked = jnp.concatenate(rows + [jnp.zeros((9, D), F32)], axis=0)
        terms[layer, 7 * D : 7 * D + 16, :] = stacked.astype(BF16)

    def reduce_start(layer):
        copies = []
        for step in range(1, ny):
            peer = lax.rem(b + step, ny)
            rows = pl.ds(pl.multiple_of(peer * chunk, chunk), chunk)
            copies.append(
                remote(
                    terms.at[layer, rows], rs_in.at[layer, step - 1],
                    rs_s.at[layer, step - 1], rs_r.at[layer, step - 1], (a, peer),
                )
            )
        for copy in copies:
            copy.start()
        everything.extend(copies)
        return copies

    def exchange_start(layer, arriving):
        landed(arriving)
        total = terms[layer, pl.ds(pl.multiple_of(b * chunk, chunk), chunk), :].astype(F32)
        for step in range(ny - 1):
            total = total + rs_in[layer, step].astype(F32)
        ar_buf[layer, a] = total.astype(BF16)
        out, come = [], []
        for step in range(1, nx):
            peer = lax.rem(a + step, nx)
            source = lax.rem(a + (nx - step), nx)
            sems = (ar_s.at[layer, step - 1], ar_r.at[layer, step - 1])
            out.append(remote(ar_buf.at[layer, a], ar_buf.at[layer, a], *sems, (peer, b)))
            come.append(remote(ar_buf.at[layer, source], ar_buf.at[layer, source], *sems, (peer, b)))
        for copy in out:
            copy.start()
        everything.extend(out)
        return come

    def spread_start(layer, arriving):
        landed(arriving)
        total = ar_buf[layer, 0].astype(F32)
        for step in range(1, nx):
            total = total + ar_buf[layer, step].astype(F32)
        final[layer, b] = total.astype(BF16)
        out, come = [], []
        for step in range(1, ny):
            peer = lax.rem(b + step, ny)
            source = lax.rem(b + (ny - step), ny)
            sems = (ag_s.at[layer, step - 1], ag_r.at[layer, step - 1])
            out.append(remote(final.at[layer, b], final.at[layer, b], *sems, (a, peer)))
            come.append(remote(final.at[layer, source], final.at[layer, source], *sems, (a, peer)))
        for copy in out:
            copy.start()
        everything.extend(out)
        return come

    def spread_finish(layer, arriving):
        landed(arriving)
        summed = final[layer].reshape(GRAD_ROWS, D).astype(F32)
        for index in range(2):
            gein_o[layer, index] = summed[index * D : index * D + D]
            gehid_o[layer, index] = summed[(index + 2) * D : (index + 3) * D]
            gnin_o[layer, index] = summed[(index + 4) * D : (index + 5) * D]
        gnout_o[layer] = summed[6 * D : 7 * D]
        gbia_o[layer] = summed[7 * D : 7 * D + 5]
        ggai_o[layer] = summed[7 * D + 5 : 7 * D + 7]

    def backward(layer, cotangent, before_edges):
        own = state[layer]
        normed = xh2s[layer]
        lifted = cotangent * gain(layer, 1)
        grad_gain_node = jnp.sum(cotangent * normed, axis=0, keepdims=True)
        inner = jnp.mean(lifted * normed, axis=1, keepdims=True)
        grad = rs2s[layer] * (lifted - jnp.mean(lifted, axis=1, keepdims=True) - normed * inner)
        grad_b4 = jnp.sum(grad, axis=0, keepdims=True)
        grad = grad.astype(BF16)
        put_term(layer, 6, dot_tn(nhs[layer], grad))
        grad = dot_nt(grad, n_out[layer]) * (d3s[layer] * 0.5)
        grad_b3 = jnp.sum(grad, axis=0, keepdims=True)
        grad = grad.astype(BF16)
        put_term(layer, 4, dot_tn(own, grad))
        put_term(layer, 5, dot_tn(agg[layer], grad))
        own_grad = cotangent + dot_nt(grad, n_in[layer, 0])
        grad_agg = dot_nt(grad, n_in[layer, 1])
        grad_gain_edge = jnp.sum(grad_agg * agg_raw[layer], axis=0, keepdims=True)
        lifted = grad_agg * gain(layer, 0)
        dxc[...] = lifted - jnp.mean(lifted, axis=1, keepdims=True)
        g_recv[...] = jnp.zeros((ROWS, D), F32)
        dsend[...] = jnp.zeros((HALF, 2 * D), F32)
        dw_out[...] = jnp.zeros((D, D), F32)
        dw_mid[...] = jnp.zeros((D, D), F32)
        db_out[...] = jnp.zeros((8, 2 * D), F32)
        db_mid[...] = jnp.zeros((8, 2 * D), F32)
        before_edges()

        def pair(j, carry):
            for first in range(0, ROWS, BLOCK):
                rows = slice(first, first + BLOCK)
                lift = twice(dxc[rows])
                unit = xhs[layer, j, rows].astype(F32)
                shared = dot((lift * unit).astype(BF16), ones[...])
                grad = rss[layer, j, rows].astype(F32) * (lift - unit * shared)
                db_out[...] += partial_sums(grad)
                grad = grad.astype(BF16)
                hidden = h2s[layer, j, rows]
                dw_out[...] += dot_tn(hidden[:, :D], grad[:, :D]) + dot_tn(hidden[:, D:], grad[:, D:])
                grad = dot(grad, w_out_t[layer]) * d2s[layer, j, rows].astype(F32)
                db_mid[...] += partial_sums(grad)
                grad = grad.astype(BF16)
                hidden = h1s[layer, j, rows]
                dw_mid[...] += dot_tn(hidden[:, :D], grad[:, :D]) + dot_tn(hidden[:, D:], grad[:, D:])
                grad = dot(grad, w_mid_t[layer]) * d1s[layer, j, rows].astype(F32)
                g_recv[rows] += grad[:, :D] + grad[:, D:]
                for part in range(2):
                    piece = grad[:, part * D : part * D + D]
                    high = upper[j + part * PAIRS, rows] > 0.5
                    split = jnp.concatenate([jnp.where(high, 0.0, piece), jnp.where(high, piece, 0.0)], axis=1)
                    g_rows[part, rows] = split.astype(BF16)
            dsend[...] += dot(hits_t[j], g_rows[0]) + dot(hits_t[j + PAIRS], g_rows[1])
            return carry

        lax.fori_loop(0, PAIRS, pair, 0)
        send_grad = dsend[...].astype(BF16)
        low = send_grad[:, :D]
        high_own = send_grad[: ROWS - HALF, D:]
        high_halo = send_grad[ROWS - HALF :, D:]
        ret_out[layer] = dot_nt(high_halo, e_in[layer, 1]).astype(BF16)
        returning = swap_halo(ret_out.at[layer], ret_in.at[layer], ret_s.at[layer], ret_r.at[layer], -1)
        everything.extend(returning)
        send_own = jnp.concatenate([low, high_own], axis=0)
        term = dot_tn(own, send_own) + dot_tn(halo_in[layer], high_halo)
        put_term(layer, 1, term)
        grad = g_recv[...]
        grad_b0 = jnp.sum(grad, axis=0, keepdims=True)
        grad = grad.astype(BF16)
        put_term(layer, 0, dot_tn(own, grad))
        put_term(layer, 2, dw_mid[...])
        put_term(layer, 3, dw_out[...])
        total_mid = jnp.sum(db_mid[...], axis=0, keepdims=True)
        total_out = jnp.sum(db_out[...], axis=0, keepdims=True)
        put_rows(
            layer,
            [
                grad_b0,
                total_mid[:, :D] + total_mid[:, D:],
                total_out[:, :D] + total_out[:, D:],
                grad_b3,
                grad_b4,
                grad_gain_edge,
                grad_gain_node,
            ],
        )
        reducing = reduce_start(layer)
        own_grad = own_grad + dot_nt(grad, e_in[layer, 0]) + dot_nt(send_own, e_in[layer, 1])
        landed(returning)
        own_grad = own_grad + dot(pick_back[...], ret_in[layer])
        return own_grad.astype(BF16), reducing

    rounded, reducing_top = backward(1, gout[...].astype(F32), lambda: None)
    exchanging = []
    rounded, reducing_low = backward(
        0, rounded.astype(F32), lambda: exchanging.extend(exchange_start(1, reducing_top))
    )
    spreading_top = spread_start(1, exchanging)

    back_target = jnp.where(from_row == 4.0, -1.0, from_row * CAP + aslot_row)
    back_out[...] = dot(one_hot_rows(back_target, SLOTS), rounded).astype(BF16)
    going_back = swap_slots(back_out, back_in, back_s, back_r, -1)
    everything += going_back
    exchange_low = exchange_start(0, reducing_low)
    stay_pick = one_hot_lanes(column(jnp.where(to_row == 4.0, slot_row, -1.0)), ROWS)
    come_pick = one_hot_lanes(column(out_target), POOL)
    staying = dot(stay_pick, rounded)
    landed(going_back)
    glat_o[...] = (staying + dot(come_pick, back_in[...])).astype(BF16)
    spreading_low = spread_start(0, exchange_low)
    spread_finish(1, spreading_top)
    spread_finish(0, spreading_low)
    for copy in everything:
        copy.wait_send()


def shards(
    latent, move_to, move_slot, arrive_from, arrive_slot, neighbours, valid_count, face_send, corner_send,
    edge_in, edge_hid, node_in, node_out, biases, gains, grad_out,
):
    nx, ny = lax.axis_size("bx"), lax.axis_size("by")
    chunk = GRAD_ROWS // ny
    vmem = pl.BlockSpec(memory_space=pltpu.VMEM)
    shape = jax.ShapeDtypeStruct
    saved = pltpu.VMEM((LAYERS, PAIRS, ROWS, 2 * D), BF16)
    node = pltpu.VMEM((LAYERS, ROWS, D), F32)
    node_bf = pltpu.VMEM((LAYERS, ROWS, D), BF16)
    wide = pltpu.VMEM((LAYERS, 2 * D, 2 * D), BF16)
    dma = pltpu.SemaphoreType.DMA
    scratch = dict(
        outgoing=pltpu.VMEM((SLOTS, D), BF16),
        arrived=pltpu.VMEM((POOL, D), BF16),
        halo_out=pltpu.VMEM((LAYERS, HALO, D), BF16),
        halo_in=pltpu.VMEM((LAYERS, HALO, D), BF16),
        ret_out=pltpu.VMEM((LAYERS, HALO, D), BF16),
        ret_in=pltpu.VMEM((LAYERS, HALO, D), BF16),
        back_out=pltpu.VMEM((SLOTS, D), BF16),
        back_in=pltpu.VMEM((POOL, D), BF16),
        pick_send=pltpu.VMEM((HALO, ROWS), BF16),
        pick_back=pltpu.VMEM((ROWS, HALO), BF16),
        hits=pltpu.VMEM((K, ROWS, ROWS), BF16),
        hits_t=pltpu.VMEM((K, HALF, ROWS), BF16),
        upper=pltpu.VMEM((K, ROWS, D), F32),
        count_col=pltpu.VMEM((ROWS, D), F32),
        state=node_bf,
        recv_term=pltpu.VMEM((ROWS, D), F32),
        send_tab=pltpu.VMEM((ROWS, 2 * D), BF16),
        w_mid=wide,
        w_out=wide,
        w_mid_t=wide,
        w_out_t=wide,
        ones=pltpu.VMEM((2 * D, 2 * D), BF16),
        h1s=saved,
        h2s=saved,
        d1s=saved,
        d2s=saved,
        xhs=saved,
        rss=saved,
        acc=pltpu.VMEM((ROWS, D), F32),
        agg=node_bf,
        nhs=node_bf,
        d3s=node,
        xh2s=node,
        rs2s=node,
        dxc=pltpu.VMEM((ROWS, D), F32),
        g_rows=pltpu.VMEM((2, ROWS, 2 * D), BF16),
        g_recv=pltpu.VMEM((ROWS, D), F32),
        agg_raw=node,
        dsend=pltpu.VMEM((HALF, 2 * D), F32),
        dw_out=pltpu.VMEM((D, D), F32),
        dw_mid=pltpu.VMEM((D, D), F32),
        db_out=pltpu.VMEM((8, 2 * D), F32),
        db_mid=pltpu.VMEM((8, 2 * D), F32),
        terms=pltpu.VMEM((LAYERS, GRAD_ROWS, D), BF16),
        rs_in=pltpu.VMEM((LAYERS, ny - 1, chunk, D), BF16),
        ar_buf=pltpu.VMEM((LAYERS, nx, chunk, D), BF16),
        final=pltpu.VMEM((LAYERS, ny, chunk, D), BF16),
        mig_s=dma((CODES,)),
        mig_r=dma((CODES,)),
        halo_s=dma((LAYERS, 8)),
        halo_r=dma((LAYERS, 8)),
        ret_s=dma((LAYERS, 8)),
        ret_r=dma((LAYERS, 8)),
        back_s=dma((CODES,)),
        back_r=dma((CODES,)),
        rs_s=dma((LAYERS, ny - 1)),
        rs_r=dma((LAYERS, ny - 1)),
        ar_s=dma((LAYERS, nx - 1)),
        ar_r=dma((LAYERS, nx - 1)),
        ag_s=dma((LAYERS, ny - 1)),
        ag_r=dma((LAYERS, ny - 1)),
    )

    def row(values):
        return values.reshape(1, ROWS)

    return pl.pallas_call(
        functools.partial(kernel, nx, ny),
        out_shape=(
            shape((ROWS, D), BF16),
            shape((ROWS, D), BF16),
            shape((LAYERS, 2, D, D), F32),
            shape((LAYERS, 2, D, D), F32),
            shape((LAYERS, 2, D, D), F32),
            shape((LAYERS, D, D), F32),
            shape((LAYERS, 5, D), F32),
            shape((LAYERS, 2, D), F32),
        ),
        in_specs=[vmem] * 16,
        out_specs=(vmem,) * 8,
        scratch_shapes=list(scratch.values()),
        compiler_params=pltpu.CompilerParams(
            collective_id=0, has_side_effects=True, vmem_limit_bytes=60 * 1024 * 1024
        ),
        name="evolve",
    )(
        latent, row(move_to), row(move_slot), row(arrive_from), row(arrive_slot),
        neighbours.T, row(valid_count), face_send.reshape(4, -1), corner_send.reshape(4, -1),
        edge_in, edge_hid, node_in, node_out, biases.transpose(1, 0, 2), gains, grad_out,
    )


def solution(mesh):
    both = ("bx", "by")
    rows, wide, grid = P(both), P(both, None), P("bx", "by", None, None)
    return jax.shard_map(
        shards,
        mesh=mesh,
        in_specs=(wide, rows, rows, rows, rows, wide, rows, grid, grid, P(), P(), P(), P(), P(), P(), wide),
        out_specs=(wide, wide, P(), P(), P(), P(), P(), P()),
        check_vma=False,
    )
```

time: 566 us -> 110 us (0.19); the launches traced: 554 us -> 110 us
  waiting for transfers between devices: 165 us -> 0 us
  matrix products: 105 us -> 0 us
  Pallas kernels: 0 us -> 101 us
  local copies, waits for them, and re-layouts: 83.9 us -> 7.89 us
  blocking collectives: 64.3 us -> 0 us
  other arithmetic: 63.2 us -> 0 us
  starting transfers between devices: 53.9 us -> 0 us
  between operations: 16.2 us -> 0.67 us
    psum x1 -> x0, waiting for transfers between devices: 144 us -> none  [shards(): lax.psum((stacked[0], stacked[1], stacked[2], stacked[3], stacked[4], sta...]
    dot_general x78 -> x0, matrix products: 105 us -> none  [the longest x16 24.9 us: edge_block(): jnp.dot(hidden_two, w_out, preferred_element_type=jnp.float32) + bias_out]
    pallas_call x0 -> x1, Pallas kernels: none -> 101 us  [shards(): pl.pallas_call(functools.partial(kernel, nx, ny), out_shape=(shape((ROWS,...]
    psum x1 -> x0, blocking collectives: 64.3 us -> none  [shards(): lax.psum((stacked[0], stacked[1], stacked[2], stacked[3], stacked[4], sta...]
    ppermute x24 -> x0, starting transfers between devices: 53.9 us -> none  [from_behind(): return lax.ppermute(value, axis, pairs)]
    reduce_sum x36 -> x0, other arithmetic: 29.2 us -> none  [the longest x4 7.81 us: edge_block(): return jnp.sum(jnp.where(live[:, :, None], message, 0.0), axis=1)]
    while x176 -> x0, local copies, waits for them, and re-layouts: 22.4 us -> none
    convert_element_type x18 -> x0, other arithmetic: 22.2 us -> none  [the longest x8 15.9 us: split_pair(): low = (values - high.astype(jnp.float32)).astype(jnp.bfloat16)]
  transfers between devices with their start and end apart: 25 -> 0, of which waited for: 14 -> 0; matrix products, arithmetic and copies ran while one was open for 4% -> 0% of each run, Pallas kernels for 0% -> 0%
where the time goes in v1:
time: 110 us
  Pallas kernels  101 us (92%)
  local copies, waits for them, and re-layouts  7.89 us (7%)
    pallas_call x1, Pallas kernels, shards(): pl.pallas_call(functools.partial(kernel, nx, ny), out_shape=(shape((ROWS,...  101 us
    unnamed x21, local copies, waits for them, and re-layouts  7.29 us

profile of v1, /device:TPU:1, one launch (start us, length us, event | category | flops | bytes accessed | tf_op | source)
XLA Modules:
  0.0 110.0 jit_solution(4111328040296288705)
XLA Ops:
  0.6 101.5 %evolve.1 = (bf16[512,128]{1,0:T(8,128)(2,1)}, bf16[512,128]{1,0:T(8,128)(2,1)}, f32[2,2,128,128]{3,2,1,0:T(8,128)}, f32[2,2,128,128]{3,2,1,0:T(8,128)}, f32[2,2...) custom-call(bf16[512,128]{1,0:T(8,128)(2,1)} %lat.1, ...), custom_call_target="tpu_custom_call" | custom-call | tf_op jit(solution)/shard_map/evolve/pallas_call | solution.py:555
  102.1 0.0 copy-start.5
  102.1 0.7 copy-done.5
  102.8 0.0 copy-start.4
  102.8 0.6 copy.24
  103.4 0.0 copy-start.2
  103.4 1.6 %copy.32 = bf16[512,128]{1,0:T(8,128)(2,1)} copy(bf16[512,128]{1,0:T(8,128)(2,1)} %get-tuple-element.24) | data formatting | bytes 262144
  105.0 0.0 copy-done.4
  105.0 0.7 copy.33
  105.7 0.0 copy-done.2
  105.7 0.0 copy-start.1
  105.7 0.7 copy.34
  106.4 0.3 copy-done.1
  106.7 0.0 copy-start
  106.7 0.7 copy.35
  107.4 0.3 copy-done
  107.8 0.0 copy-start.3
  107.8 0.7 copy.36
  108.5 0.3 copy-done.3
  108.8 0.0 copy-start.6
  108.8 0.7 copy.37
  109.4 0.0 copy-done.6
  109.5 0.6 copy.38
Async XLA Ops:
  102.1 0.7 copy-start.5
  102.8 2.2 %copy-start.4 = (bf16[512,128]{1,0:T(8,128)(2,1)S(1)}, bf16[512,128]{1,0:T(8,128)(2,1)}, u32[]{:S(2)}) copy-start(bf16[512,128]{1,0:T(8,128)(2,1)} %get-tuple-element.25) | copy-start | bytes 393220
  103.4 2.3 %copy-start.2 = (f32[2,2,128,128]{3,2,1,0:T(8,128)S(1)}, f32[2,2,128,128]{3,2,1,0:T(8,128)}, u32[]{:S(2)}) copy-start(f32[2,2,128,128]{3,2,1,0:T(8,128)} %get-tuple-element.26) | copy-start | bytes 786436
  105.7 1.0 copy-start.1
  106.7 1.0 copy-start
  107.8 1.0 copy-start.3
  108.8 0.7 copy-start.6

commit v2 on v1

--- a/solution.py
+++ b/solution.py
@@ -19,7 +19,9 @@
 SLOTS = CODES * CAP
 POOL = 384
 GRAD_ROWS = 1024
-BLOCK = 256
+BLOCK = 512
+FORWARD_PAIRS = 4
+BACKWARD_PAIRS = 4
 F32 = jnp.float32
 BF16 = jnp.bfloat16
 MESH = pl.DeviceIdType.MESH
@@ -73,6 +75,21 @@
     return jnp.sum(values.reshape(values.shape[0] // 8, 8, values.shape[1]), axis=0)
 
 
+def staggered(chain, pairs):
+    def body(group, carry):
+        waiting = [
+            chain(group * pairs + pair, first) for pair in range(pairs) for first in range(0, ROWS, BLOCK)
+        ]
+        running = []
+        while waiting or running:
+            if waiting:
+                running.append(waiting.pop(0))
+            running = [one for one in running if next(one, True) is None]
+        return carry
+
+    lax.fori_loop(0, PAIRS // pairs, body, 0)
+
+
 def layer_norm_parts(values):
     centred = values - jnp.mean(values, axis=1, keepdims=True)
     scale = lax.rsqrt(jnp.mean(centred * centred, axis=1, keepdims=True) + 1e-05)
@@ -95,7 +112,7 @@
     pick_send, pick_back, hits, hits_t, upper, count_col,
     state, recv_term, send_tab, w_mid, w_out, w_mid_t, w_out_t, ones,
     h1s, h2s, d1s, d2s, xhs, rss, acc, agg, nhs, d3s, xh2s, rs2s,
-    dxc, g_rows, g_recv, agg_raw, dsend, dw_out, dw_mid, db_out, db_mid,
+    dxc, g_recv, agg_raw, dsend, dw_out, dw_mid, db_out, db_mid,
     terms, rs_in, ar_buf, final,
     mig_s, mig_r, halo_s, halo_r, ret_s, ret_r, back_s, back_r,
     rs_s, rs_r, ar_s, ar_r, ag_s, ag_r,
@@ -236,35 +253,40 @@
         landed(halo)
         send_tab[ROWS - HALF : HALF, D:] = dot(halo_in[layer], w_send).astype(BF16)
 
-        def pair(j, carry):
-            low_slot = j.astype(F32)
-            for first in range(0, ROWS, BLOCK):
-                rows = slice(first, first + BLOCK)
-                parts = []
-                for k in (j, j + PAIRS):
-                    both = dot(hits[k, rows], send_tab[...])
-                    parts.append(recv_term[rows] + jnp.where(upper[k, rows] > 0.5, both[:, D:], both[:, :D]))
-                value, slope = half_silu(jnp.concatenate(parts, axis=1))
-                value = value.astype(BF16)
-                h1s[layer, j, rows] = value
-                d1s[layer, j, rows] = slope.astype(BF16)
-                value, slope = half_silu(dot(value, w_mid[layer]) + bias_mid)
-                value = value.astype(BF16)
-                h2s[layer, j, rows] = value
-                d2s[layer, j, rows] = slope.astype(BF16)
-                centred = dot(value, w_out[layer]) + bias_out
-                variance = dot((centred * centred).astype(BF16), ones[...])
-                scale = lax.rsqrt(variance + 1e-05)
-                live = count_col[rows]
-                mask = jnp.concatenate([live > low_slot, live > low_slot + PAIRS], axis=1)
-                scale = jnp.where(mask, scale, 0.0)
-                normed = centred * scale
-                rss[layer, j, rows] = scale.astype(BF16)
-                xhs[layer, j, rows] = normed.astype(BF16)
-                acc[rows] += normed[:, :D] + normed[:, D:]
-            return carry
-
-        lax.fori_loop(0, PAIRS, pair, 0)
+        def chain(j, first):
+            rows = slice(first, first + BLOCK)
+            both = [dot(hits[k, rows], send_tab[...]) for k in (j, j + PAIRS)]
+            yield
+            parts = [
+                recv_term[rows] + jnp.where(upper[k, rows] > 0.5, pick[:, D:], pick[:, :D])
+                for k, pick in zip((j, j + PAIRS), both)
+            ]
+            value, slope = half_silu(jnp.concatenate(parts, axis=1))
+            value = value.astype(BF16)
+            h1s[layer, j, rows] = value
+            d1s[layer, j, rows] = slope.astype(BF16)
+            product = dot(value, w_mid[layer])
+            yield
+            value, slope = half_silu(product + bias_mid)
+            value = value.astype(BF16)
+            h2s[layer, j, rows] = value
+            d2s[layer, j, rows] = slope.astype(BF16)
+            product = dot(value, w_out[layer])
+            yield
+            centred = product + bias_out
+            variance = dot((centred * centred).astype(BF16), ones[...])
+            yield
+            scale = lax.rsqrt(variance + 1e-05)
+            live = count_col[rows]
+            low_slot = jnp.float32(j) if isinstance(j, int) else j.astype(F32)
+            mask = jnp.concatenate([live > low_slot, live > low_slot + PAIRS], axis=1)
+            scale = jnp.where(mask, scale, 0.0)
+            normed = centred * scale
+            rss[layer, j, rows] = scale.astype(BF16)
+            xhs[layer, j, rows] = normed.astype(BF16)
+            acc[rows] += normed[:, :D] + normed[:, D:]
+
+        staggered(chain, FORWARD_PAIRS)
         total = acc[...]
         agg_raw[layer] = total
         total = (total * gain(layer, 0)).astype(BF16)
@@ -385,33 +407,39 @@
         db_mid[...] = jnp.zeros((8, 2 * D), F32)
         before_edges()
 
-        def pair(j, carry):
-            for first in range(0, ROWS, BLOCK):
-                rows = slice(first, first + BLOCK)
-                lift = twice(dxc[rows])
-                unit = xhs[layer, j, rows].astype(F32)
-                shared = dot((lift * unit).astype(BF16), ones[...])
-                grad = rss[layer, j, rows].astype(F32) * (lift - unit * shared)
-                db_out[...] += partial_sums(grad)
-                grad = grad.astype(BF16)
-                hidden = h2s[layer, j, rows]
-                dw_out[...] += dot_tn(hidden[:, :D], grad[:, :D]) + dot_tn(hidden[:, D:], grad[:, D:])
-                grad = dot(grad, w_out_t[layer]) * d2s[layer, j, rows].astype(F32)
-                db_mid[...] += partial_sums(grad)
-                grad = grad.astype(BF16)
-                hidden = h1s[layer, j, rows]
-                dw_mid[...] += dot_tn(hidden[:, :D], grad[:, :D]) + dot_tn(hidden[:, D:], grad[:, D:])
-                grad = dot(grad, w_mid_t[layer]) * d1s[layer, j, rows].astype(F32)
-                g_recv[rows] += grad[:, :D] + grad[:, D:]
-                for part in range(2):
-                    piece = grad[:, part * D : part * D + D]
-                    high = upper[j + part * PAIRS, rows] > 0.5
-                    split = jnp.concatenate([jnp.where(high, 0.0, piece), jnp.where(high, piece, 0.0)], axis=1)
-                    g_rows[part, rows] = split.astype(BF16)
-            dsend[...] += dot(hits_t[j], g_rows[0]) + dot(hits_t[j + PAIRS], g_rows[1])
-            return carry
-
-        lax.fori_loop(0, PAIRS, pair, 0)
+        def chain(j, first):
+            rows = slice(first, first + BLOCK)
+            lift = twice(dxc[rows])
+            unit = xhs[layer, j, rows].astype(F32)
+            shared = dot((lift * unit).astype(BF16), ones[...])
+            yield
+            grad = rss[layer, j, rows].astype(F32) * (lift - unit * shared)
+            db_out[...] += partial_sums(grad)
+            grad = grad.astype(BF16)
+            product = dot(grad, w_out_t[layer])
+            hidden = h2s[layer, j, rows]
+            dw_out[...] += dot_tn(hidden[:, :D], grad[:, :D]) + dot_tn(hidden[:, D:], grad[:, D:])
+            yield
+            grad = product * d2s[layer, j, rows].astype(F32)
+            db_mid[...] += partial_sums(grad)
+            grad = grad.astype(BF16)
+            product = dot(grad, w_mid_t[layer])
+            hidden = h1s[layer, j, rows]
+            dw_mid[...] += dot_tn(hidden[:, :D], grad[:, :D]) + dot_tn(hidden[:, D:], grad[:, D:])
+            yield
+            grad = product * d1s[layer, j, rows].astype(F32)
+            g_recv[rows] += grad[:, :D] + grad[:, D:]
+            scattered = None
+            for part in range(2):
+                k = j + part * PAIRS
+                piece = grad[:, part * D : part * D + D]
+                high = upper[k, rows] > 0.5
+                split = jnp.concatenate([jnp.where(high, 0.0, piece), jnp.where(high, piece, 0.0)], axis=1)
+                added = dot(hits_t[k, :, rows], split.astype(BF16))
+                scattered = added if scattered is None else scattered + added
+            dsend[...] += scattered
+
+        staggered(chain, BACKWARD_PAIRS)
         send_grad = dsend[...].astype(BF16)
         low = send_grad[:, :D]
         high_own = send_grad[: ROWS - HALF, D:]
@@ -521,7 +549,6 @@
         xh2s=node,
         rs2s=node,
         dxc=pltpu.VMEM((ROWS, D), F32),
-        g_rows=pltpu.VMEM((2, ROWS, 2 * D), BF16),
         g_recv=pltpu.VMEM((ROWS, D), F32),
         agg_raw=node,
         dsend=pltpu.VMEM((HALF, 2 * D), F32),

time: 110 us -> 88.6 us (0.81)
  Pallas kernels: 101 us -> 79.7 us
    pallas_call x1, Pallas kernels: 101 us -> 79.7 us  [shards(): pl.pallas_call(functools.partial(kernel, nx, ny), out_shape=(shape((ROWS,...]
where the time goes in v2:
time: 88.6 us; the launch traced here: 88.3 us
  Pallas kernels  79.7 us (90%)
  local copies, waits for them, and re-layouts  7.89 us (9%)
    pallas_call x1, Pallas kernels, shards(): pl.pallas_call(functools.partial(kernel, nx, ny), out_shape=(shape((ROWS,...  79.7 us
    unnamed x21, local copies, waits for them, and re-layouts  7.29 us

profile of v2, /device:TPU:1, one launch (start us, length us, event | category | flops | bytes accessed | tf_op | source)
XLA Modules:
  0.0 88.3 jit_solution(9218479442361727616)
XLA Ops:
  0.6 79.7 %evolve.1 = (bf16[512,128]{1,0:T(8,128)(2,1)}, bf16[512,128]{1,0:T(8,128)(2,1)}, f32[2,2,128,128]{3,2,1,0:T(8,128)}, f32[2,2,128,128]{3,2,1,0:T(8,128)}, f32[2,2...) custom-call(bf16[512,128]{1,0:T(8,128)(2,1)} %lat.1, ...), custom_call_target="tpu_custom_call" | custom-call | tf_op jit(solution)/shard_map/evolve/pallas_call | solution.py:582
  80.4 0.0 copy-start.5
  80.4 0.7 copy-done.5
  81.1 0.0 copy-start.4
  81.1 0.6 copy.24
  81.7 0.0 copy-start.2
  81.7 1.6 %copy.32 = bf16[512,128]{1,0:T(8,128)(2,1)} copy(bf16[512,128]{1,0:T(8,128)(2,1)} %get-tuple-element.24) | data formatting | bytes 262144
  83.3 0.0 copy-done.4
  83.3 0.7 copy.33
  83.9 0.0 copy-done.2
  83.9 0.0 copy-start.1
  83.9 0.7 copy.34
  84.6 0.3 copy-done.1
  85.0 0.0 copy-start
  85.0 0.7 copy.35
  85.7 0.3 copy-done
  86.0 0.0 copy-start.3
  86.0 0.7 copy.36
  86.7 0.3 copy-done.3
  87.0 0.0 copy-start.6
  87.0 0.7 copy.37
  87.7 0.0 copy-done.6
  87.7 0.6 copy.38
Async XLA Ops:
  80.4 0.7 copy-start.5
  81.1 2.2 %copy-start.4 = (bf16[512,128]{1,0:T(8,128)(2,1)S(1)}, bf16[512,128]{1,0:T(8,128)(2,1)}, u32[]{:S(2)}) copy-start(bf16[512,128]{1,0:T(8,128)(2,1)} %get-tuple-element.25) | copy-start | bytes 393220
  81.7 2.3 %copy-start.2 = (f32[2,2,128,128]{3,2,1,0:T(8,128)S(1)}, f32[2,2,128,128]{3,2,1,0:T(8,128)}, u32[]{:S(2)}) copy-start(f32[2,2,128,128]{3,2,1,0:T(8,128)} %get-tuple-element.26) | copy-start | bytes 786436
  83.9 1.0 %copy-start.1 = (f32[2,2,128,128]{3,2,1,0:T(8,128)S(1)}, f32[2,2,128,128]{3,2,1,0:T(8,128)}, u32[]{:S(2)}) copy-start(f32[2,2,128,128]{3,2,1,0:T(8,128)} %get-tuple-element.27) | copy-start | bytes 786436
  85.0 1.0 %copy-start = (f32[2,2,128,128]{3,2,1,0:T(8,128)S(1)}, f32[2,2,128,128]{3,2,1,0:T(8,128)}, u32[]{:S(2)}) copy-start(f32[2,2,128,128]{3,2,1,0:T(8,128)} %get-tuple-element.28) | copy-start | bytes 786436
  86.0 1.0 %copy-start.3 = (f32[2,128,128]{2,1,0:T(8,128)S(1)}, f32[2,128,128]{2,1,0:T(8,128)}, u32[]{:S(2)}) copy-start(f32[2,128,128]{2,1,0:T(8,128)} %get-tuple-element.29) | copy-start | bytes 393220
  87.0 0.7 copy-start.6

commit v3 on v2

--- a/solution.py
+++ b/solution.py
@@ -18,7 +18,9 @@
 CODES = 9
 SLOTS = CODES * CAP
 POOL = 384
-GRAD_ROWS = 1024
+EARLY_ROWS = 1280
+LATE_ROWS = 768
+LATE_VECTORS = 512
 BLOCK = 512
 FORWARD_PAIRS = 4
 BACKWARD_PAIRS = 4
@@ -37,6 +39,22 @@
     (-1, -1, 304, 16),
 )
 
+ARGUMENTS = (
+    "lat", "move_to", "move_slot", "arrive_from", "arrive_slot", "nbr", "count", "face", "corner",
+    "e_in", "e_hid", "n_in", "n_out", "bia", "gai", "gout",
+)
+RESULTS = ("state_o", "glat_o", "early_o", "late_o")
+SCRATCH = (
+    "outgoing", "arrived", "halo_out", "halo_in", "ret_out", "ret_in", "back_out", "back_in",
+    "pick_send", "pick_back", "hits", "hits_t", "upper", "count_col", "state", "recv_term",
+    "send_tab", "w_mid", "w_out", "w_mid_t", "w_out_t", "ones", "h1s", "h2s", "d1s", "d2s", "xhs",
+    "rss", "acc", "agg", "nhs", "d3s", "xh2s", "rs2s", "dxc", "g_recv", "agg_raw", "dsend",
+    "dw_out", "dw_mid", "db_out", "db_mid", "mig_s", "mig_r", "halo_s", "halo_r", "ret_s", "ret_r",
+    "back_s", "back_r",
+)
+EDGE_GROUPS = ("late", "early")
+NODE_TERMS = (7, 4)
+
 
 def dot(a, b):
     return jnp.dot(a, b, preferred_element_type=F32)
@@ -104,22 +122,25 @@
 
 
 def kernel(
-    nx, ny,
-    lat, move_to, move_slot, arrive_from, arrive_slot, nbr, count, face, corner,
-    e_in, e_hid, n_in, n_out, bia, gai, gout,
-    state_o, glat_o, gein_o, gehid_o, gnin_o, gnout_o, gbia_o, ggai_o,
-    outgoing, arrived, halo_out, halo_in, ret_out, ret_in, back_out, back_in,
-    pick_send, pick_back, hits, hits_t, upper, count_col,
-    state, recv_term, send_tab, w_mid, w_out, w_mid_t, w_out_t, ones,
-    h1s, h2s, d1s, d2s, xhs, rss, acc, agg, nhs, d3s, xh2s, rs2s,
-    dxc, g_recv, agg_raw, dsend, dw_out, dw_mid, db_out, db_mid,
-    terms, rs_in, ar_buf, final,
-    mig_s, mig_r, halo_s, halo_r, ret_s, ret_r, back_s, back_r,
-    rs_s, rs_r, ar_s, ar_r, ag_s, ag_r,
+    nx, ny, names, *refs
 ):
+    refs = dict(zip(names, refs))
+    arguments = [(refs["arg_" + name], refs[name]) for name in ARGUMENTS]
+    (
+        lat, move_to, move_slot, arrive_from, arrive_slot, nbr, count, face, corner,
+        e_in, e_hid, n_in, n_out, bia, gai, gout,
+    ) = (local for _, local in arguments)
+    state_o, glat_o, early_o, late_o = (refs[name] for name in RESULTS)
+    (
+        outgoing, arrived, halo_out, halo_in, ret_out, ret_in, back_out, back_in,
+        pick_send, pick_back, hits, hits_t, upper, count_col,
+        state, recv_term, send_tab, w_mid, w_out, w_mid_t, w_out_t, ones,
+        h1s, h2s, d1s, d2s, xhs, rss, acc, agg, nhs, d3s, xh2s, rs2s,
+        dxc, g_recv, agg_raw, dsend, dw_out, dw_mid, db_out, db_mid,
+        mig_s, mig_r, halo_s, halo_r, ret_s, ret_r, back_s, back_r,
+    ) = (refs[name] for name in SCRATCH)
     a = lax.axis_index("bx")
     b = lax.axis_index("by")
-    chunk = GRAD_ROWS // ny
 
     def at(move_x, move_y):
         return (lax.rem(a + (move_x + nx), nx), lax.rem(b + (move_y + ny), ny))
@@ -134,6 +155,15 @@
     partners += [(1, 1), (1, -1), (-1, 1), (-1, -1)]
     for move_x, move_y in partners:
         pl.semaphore_signal(barrier, inc=1, device_id=at(move_x, move_y), device_id_type=MESH)
+
+    loads = [
+        pltpu.make_async_copy(there, here, refs["load_s"].at[index])
+        for index, (there, here) in enumerate(arguments)
+    ]
+    for load in loads:
+        load.start()
+    for load in loads[:9]:
+        load.wait()
 
     def as_row(ref):
         return ref[...].astype(F32)
@@ -195,7 +225,6 @@
     for index in range(4):
         filled = column(corner[index : index + 1, :].astype(F32))
         pick_send[256 + index * 16 : 272 + index * 16, :] = one_hot_lanes(filled, ROWS)
-    pick_back[...] = jnp.transpose(pick_send[...].astype(F32)).astype(BF16)
     count_col[...] = column(as_row(count))
 
     def build_hits(k, carry):
@@ -204,10 +233,17 @@
         inner = jnp.where(high, row - float(HALF), row)
         hits[k] = one_hot_lanes(column(inner), ROWS)
         upper[k] = column(jnp.where(high, 1.0, 0.0))
-        hits_t[k] = one_hot_rows(inner, HALF)
         return carry
 
     lax.fori_loop(0, K, build_hits, 0)
+
+    def build_hits_t(k, carry):
+        row = nbr[pl.ds(k, 1), :].astype(F32)
+        hits_t[k] = one_hot_rows(jnp.where(row >= float(HALF), row - float(HALF), row), HALF)
+        return carry
+
+    for load in loads[9:]:
+        load.wait()
 
     diag = (lax.broadcasted_iota(jnp.int32, (2 * D, 2 * D), 0) // D) == (
         lax.broadcasted_iota(jnp.int32, (2 * D, 2 * D), 1) // D
@@ -222,9 +258,7 @@
         mid = e_hid[layer, 0].astype(F32) * 0.5
         out = e_hid[layer, 1].astype(F32)
         w_mid[layer] = doubled(mid)
-        w_mid_t[layer] = doubled(jnp.transpose(mid))
         w_out[layer] = doubled(out - jnp.mean(out, axis=1, keepdims=True))
-        w_out_t[layer] = doubled(jnp.transpose(out) * 0.5)
     send_tab[HALF:, :] = jnp.zeros((ROWS - HALF, 2 * D), BF16)
 
     def bias(layer, index):
@@ -233,10 +267,19 @@
     def gain(layer, index):
         return gai[layer, index : index + 1, :]
 
+    def later_uses():
+        lax.fori_loop(0, K, build_hits_t, 0)
+        pick_back[...] = jnp.transpose(pick_send[...].astype(F32)).astype(BF16)
+
+    def later_weights():
+        for layer in range(LAYERS):
+            w_mid_t[layer] = doubled(jnp.transpose(e_hid[layer, 0].astype(F32)) * 0.5)
+            w_out_t[layer] = doubled(jnp.transpose(e_hid[layer, 1].astype(F32)) * 0.5)
+
     landed(migration)
     state[0] = (staying + dot(come_pick, arrived[...])).astype(BF16)
 
-    def forward(layer):
+    def forward(layer, meanwhile):
         halo_out[layer] = dot(pick_send[...], state[layer]).astype(BF16)
         halo = swap_halo(halo_out.at[layer], halo_in.at[layer], halo_s.at[layer], halo_r.at[layer], 1)
         everything.extend(halo)
@@ -250,6 +293,7 @@
         bias_mid = twice(bias(layer, 1)) * 0.5
         bias_out = bias(layer, 2)
         bias_out = twice(bias_out - jnp.mean(bias_out, axis=1, keepdims=True))
+        meanwhile()
         landed(halo)
         send_tab[ROWS - HALF : HALF, D:] = dot(halo_in[layer], w_send).astype(BF16)
 
@@ -302,84 +346,71 @@
         return (own.astype(F32) + normed * gain(layer, 1)).astype(BF16)
 
     for layer in range(LAYERS):
-        following = forward(layer)
+        following = forward(layer, (later_uses, later_weights)[layer])
         if layer + 1 < LAYERS:
             state[layer + 1] = following
         else:
             state_o[...] = following
 
-    def put_term(layer, index, values):
-        terms[layer, index * D : index * D + D, :] = values.astype(BF16)
-
-    def put_rows(layer, rows):
-        terms[layer, 7 * D :, :] = jnp.zeros((D, D), BF16)
-        stacked = jnp.concatenate(rows + [jnp.zeros((9, D), F32)], axis=0)
-        terms[layer, 7 * D : 7 * D + 16, :] = stacked.astype(BF16)
-
-    def reduce_start(layer):
+    def put_term(group, index, values):
+        refs["terms_" + group][index * D : index * D + D, :] = values.astype(BF16)
+
+    def reduce_start(group):
+        terms, arriving = refs["terms_" + group], refs["rs_in_" + group]
+        chunk = arriving.shape[1]
         copies = []
         for step in range(1, ny):
             peer = lax.rem(b + step, ny)
             rows = pl.ds(pl.multiple_of(peer * chunk, chunk), chunk)
-            copies.append(
-                remote(
-                    terms.at[layer, rows], rs_in.at[layer, step - 1],
-                    rs_s.at[layer, step - 1], rs_r.at[layer, step - 1], (a, peer),
-                )
-            )
+            sems = (refs["rs_s_" + group].at[step - 1], refs["rs_r_" + group].at[step - 1])
+            copies.append(remote(terms.at[rows], arriving.at[step - 1], *sems, (a, peer)))
         for copy in copies:
             copy.start()
         everything.extend(copies)
         return copies
 
-    def exchange_start(layer, arriving):
-        landed(arriving)
-        total = terms[layer, pl.ds(pl.multiple_of(b * chunk, chunk), chunk), :].astype(F32)
+    def exchange_start(group, reducing):
+        terms, arriving, summed = refs["terms_" + group], refs["rs_in_" + group], refs["ar_buf_" + group]
+        chunk = arriving.shape[1]
+        landed(reducing)
+        total = terms[pl.ds(pl.multiple_of(b * chunk, chunk), chunk), :].astype(F32)
         for step in range(ny - 1):
-            total = total + rs_in[layer, step].astype(F32)
-        ar_buf[layer, a] = total.astype(BF16)
+            total = total + arriving[step].astype(F32)
+        summed[a] = total.astype(BF16)
         out, come = [], []
         for step in range(1, nx):
             peer = lax.rem(a + step, nx)
             source = lax.rem(a + (nx - step), nx)
-            sems = (ar_s.at[layer, step - 1], ar_r.at[layer, step - 1])
-            out.append(remote(ar_buf.at[layer, a], ar_buf.at[layer, a], *sems, (peer, b)))
-            come.append(remote(ar_buf.at[layer, source], ar_buf.at[layer, source], *sems, (peer, b)))
+            sems = (refs["ar_s_" + group].at[step - 1], refs["ar_r_" + group].at[step - 1])
+            out.append(remote(summed.at[a], summed.at[a], *sems, (peer, b)))
+            come.append(remote(summed.at[source], summed.at[source], *sems, (peer, b)))
         for copy in out:
             copy.start()
         everything.extend(out)
         return come
 
-    def spread_start(layer, arriving):
-        landed(arriving)
-        total = ar_buf[layer, 0].astype(F32)
+    def spread_start(group, exchanging):
+        summed, final = refs["ar_buf_" + group], refs["final_" + group]
+        landed(exchanging)
+        total = summed[0].astype(F32)
         for step in range(1, nx):
-            total = total + ar_buf[layer, step].astype(F32)
-        final[layer, b] = total.astype(BF16)
+            total = total + summed[step].astype(F32)
+        final[b] = total.astype(BF16)
         out, come = [], []
         for step in range(1, ny):
             peer = lax.rem(b + step, ny)
             source = lax.rem(b + (ny - step), ny)
-            sems = (ag_s.at[layer, step - 1], ag_r.at[layer, step - 1])
-            out.append(remote(final.at[layer, b], final.at[layer, b], *sems, (a, peer)))
-            come.append(remote(final.at[layer, source], final.at[layer, source], *sems, (a, peer)))
+            sems = (refs["ag_s_" + group].at[step - 1], refs["ag_r_" + group].at[step - 1])
+            out.append(remote(final.at[b], final.at[b], *sems, (a, peer)))
+            come.append(remote(final.at[source], final.at[source], *sems, (a, peer)))
         for copy in out:
             copy.start()
         everything.extend(out)
         return come
 
-    def spread_finish(layer, arriving):
-        landed(arriving)
-        summed = final[layer].reshape(GRAD_ROWS, D).astype(F32)
-        for index in range(2):
-            gein_o[layer, index] = summed[index * D : index * D + D]
-            gehid_o[layer, index] = summed[(index + 2) * D : (index + 3) * D]
-            gnin_o[layer, index] = summed[(index + 4) * D : (index + 5) * D]
-        gnout_o[layer] = summed[6 * D : 7 * D]
-        gbia_o[layer] = summed[7 * D : 7 * D + 5]
-        ggai_o[layer] = summed[7 * D + 5 : 7 * D + 7]
-
-    def backward(layer, cotangent, before_edges):
+    vectors = []
+
+    def backward(layer, cotangent, before_edges, after_terms):
         own = state[layer]
         normed = xh2s[layer]
         lifted = cotangent * gain(layer, 1)
@@ -388,12 +419,12 @@
         grad = rs2s[layer] * (lifted - jnp.mean(lifted, axis=1, keepdims=True) - normed * inner)
         grad_b4 = jnp.sum(grad, axis=0, keepdims=True)
         grad = grad.astype(BF16)
-        put_term(layer, 6, dot_tn(nhs[layer], grad))
+        put_term("early", NODE_TERMS[layer] + 2, dot_tn(nhs[layer], grad))
         grad = dot_nt(grad, n_out[layer]) * (d3s[layer] * 0.5)
         grad_b3 = jnp.sum(grad, axis=0, keepdims=True)
         grad = grad.astype(BF16)
-        put_term(layer, 4, dot_tn(own, grad))
-        put_term(layer, 5, dot_tn(agg[layer], grad))
+        put_term("early", NODE_TERMS[layer], dot_tn(own, grad))
+        put_term("early", NODE_TERMS[layer] + 1, dot_tn(agg[layer], grad))
         own_grad = cotangent + dot_nt(grad, n_in[layer, 0])
         grad_agg = dot_nt(grad, n_in[layer, 1])
         grad_gain_edge = jnp.sum(grad_agg * agg_raw[layer], axis=0, keepdims=True)
@@ -449,55 +480,87 @@
         everything.extend(returning)
         send_own = jnp.concatenate([low, high_own], axis=0)
         term = dot_tn(own, send_own) + dot_tn(halo_in[layer], high_halo)
-        put_term(layer, 1, term)
+        group = EDGE_GROUPS[layer]
+        put_term(group, 1, term)
         grad = g_recv[...]
         grad_b0 = jnp.sum(grad, axis=0, keepdims=True)
         grad = grad.astype(BF16)
-        put_term(layer, 0, dot_tn(own, grad))
-        put_term(layer, 2, dw_mid[...])
-        put_term(layer, 3, dw_out[...])
+        put_term(group, 0, dot_tn(own, grad))
+        put_term(group, 2, dw_mid[...])
+        put_term(group, 3, dw_out[...])
         total_mid = jnp.sum(db_mid[...], axis=0, keepdims=True)
         total_out = jnp.sum(db_out[...], axis=0, keepdims=True)
-        put_rows(
-            layer,
-            [
-                grad_b0,
-                total_mid[:, :D] + total_mid[:, D:],
-                total_out[:, :D] + total_out[:, D:],
-                grad_b3,
-                grad_b4,
-                grad_gain_edge,
-                grad_gain_node,
-            ],
-        )
-        reducing = reduce_start(layer)
+        vectors.extend([
+            grad_b0,
+            total_mid[:, :D] + total_mid[:, D:],
+            total_out[:, :D] + total_out[:, D:],
+            grad_b3,
+            grad_b4,
+            grad_gain_edge,
+            grad_gain_node,
+        ])
+        after_terms()
         own_grad = own_grad + dot_nt(grad, e_in[layer, 0]) + dot_nt(send_own, e_in[layer, 1])
         landed(returning)
         own_grad = own_grad + dot(pick_back[...], ret_in[layer])
-        return own_grad.astype(BF16), reducing
-
-    rounded, reducing_top = backward(1, gout[...].astype(F32), lambda: None)
-    exchanging = []
-    rounded, reducing_low = backward(
-        0, rounded.astype(F32), lambda: exchanging.extend(exchange_start(1, reducing_top))
-    )
-    spreading_top = spread_start(1, exchanging)
+        return own_grad.astype(BF16)
+
+    sums = {}
+
+    def early_start():
+        sums["early"] = reduce_start("early")
+
+    def late_start():
+        terms = refs["terms_late"]
+        terms[LATE_VECTORS:, :] = jnp.zeros((LATE_ROWS - LATE_VECTORS, D), BF16)
+        stacked = jnp.concatenate(vectors + [jnp.zeros((2, D), F32)], axis=0)
+        terms[LATE_VECTORS : LATE_VECTORS + 16, :] = stacked.astype(BF16)
+        sums["late"] = reduce_start("late")
+        sums["early"] = exchange_start("early", sums["early"])
+
+    rounded = backward(1, gout[...].astype(F32), lambda: None, lambda: None)
+    rounded = backward(0, rounded.astype(F32), early_start, late_start)
 
     back_target = jnp.where(from_row == 4.0, -1.0, from_row * CAP + aslot_row)
     back_out[...] = dot(one_hot_rows(back_target, SLOTS), rounded).astype(BF16)
     going_back = swap_slots(back_out, back_in, back_s, back_r, -1)
     everything += going_back
-    exchange_low = exchange_start(0, reducing_low)
+    sums["late"] = exchange_start("late", sums["late"])
     stay_pick = one_hot_lanes(column(jnp.where(to_row == 4.0, slot_row, -1.0)), ROWS)
     come_pick = one_hot_lanes(column(out_target), POOL)
     staying = dot(stay_pick, rounded)
+    sums["early"] = spread_start("early", sums["early"])
     landed(going_back)
     glat_o[...] = (staying + dot(come_pick, back_in[...])).astype(BF16)
-    spreading_low = spread_start(0, exchange_low)
-    spread_finish(1, spreading_top)
-    spread_finish(0, spreading_low)
+    sums["late"] = spread_start("late", sums["late"])
+    landed(sums["early"])
+    early_o[...] = refs["final_early"][...].reshape(EARLY_ROWS, D)
+    landed(sums["late"])
+    late_o[...] = refs["final_late"][...].reshape(LATE_ROWS, D)
     for copy in everything:
         copy.wait_send()
+
+
+def unpack(state, grad_latent, early, late, state_o, glat_o, gein_o, gehid_o, gnin_o, gnout_o, gbia_o, ggai_o):
+    state_o[...] = state[...]
+    glat_o[...] = grad_latent[...]
+    sums = dict(early=early, late=late)
+
+    def matrix(group, index):
+        return sums[group][index * D : index * D + D, :].astype(F32)
+
+    for layer in range(LAYERS):
+        group, node = EDGE_GROUPS[layer], NODE_TERMS[layer]
+        for index in range(2):
+            gein_o[layer, index] = matrix(group, index)
+            gehid_o[layer, index] = matrix(group, index + 2)
+            gnin_o[layer, index] = matrix("early", node + index)
+        gnout_o[layer] = matrix("early", node + 2)
+    vectors = late[LATE_VECTORS : LATE_VECTORS + 16, :].astype(F32)
+    for layer in range(LAYERS):
+        first = 7 * (LAYERS - 1 - layer)
+        gbia_o[:, layer] = vectors[first : first + 5]
+        ggai_o[layer] = vectors[first + 5 : first + 7]
 
 
 def shards(
@@ -505,7 +568,6 @@
     edge_in, edge_hid, node_in, node_out, biases, gains, grad_out,
 ):
     nx, ny = lax.axis_size("bx"), lax.axis_size("by")
-    chunk = GRAD_ROWS // ny
     vmem = pl.BlockSpec(memory_space=pltpu.VMEM)
     shape = jax.ShapeDtypeStruct
     saved = pltpu.VMEM((LAYERS, PAIRS, ROWS, 2 * D), BF16)
@@ -556,10 +618,6 @@
         dw_mid=pltpu.VMEM((D, D), F32),
         db_out=pltpu.VMEM((8, 2 * D), F32),
         db_mid=pltpu.VMEM((8, 2 * D), F32),
-        terms=pltpu.VMEM((LAYERS, GRAD_ROWS, D), BF16),
-        rs_in=pltpu.VMEM((LAYERS, ny - 1, chunk, D), BF16),
-        ar_buf=pltpu.VMEM((LAYERS, nx, chunk, D), BF16),
-        final=pltpu.VMEM((LAYERS, ny, chunk, D), BF16),
         mig_s=dma((CODES,)),
         mig_r=dma((CODES,)),
         halo_s=dma((LAYERS, 8)),
@@ -568,19 +626,47 @@
         ret_r=dma((LAYERS, 8)),
         back_s=dma((CODES,)),
         back_r=dma((CODES,)),
-        rs_s=dma((LAYERS, ny - 1)),
-        rs_r=dma((LAYERS, ny - 1)),
-        ar_s=dma((LAYERS, nx - 1)),
-        ar_r=dma((LAYERS, nx - 1)),
-        ag_s=dma((LAYERS, ny - 1)),
-        ag_r=dma((LAYERS, ny - 1)),
+        load_s=dma((16,)),
     )
+    for group, total in (("early", EARLY_ROWS), ("late", LATE_ROWS)):
+        chunk = total // ny
+        scratch["terms_" + group] = pltpu.VMEM((total, D), BF16)
+        scratch["rs_in_" + group] = pltpu.VMEM((ny - 1, chunk, D), BF16)
+        scratch["ar_buf_" + group] = pltpu.VMEM((nx, chunk, D), BF16)
+        scratch["final_" + group] = pltpu.VMEM((ny, chunk, D), BF16)
+        for stage, partners in (("rs", ny), ("ar", nx), ("ag", ny)):
+            scratch[f"{stage}_s_{group}"] = dma((partners - 1,))
+            scratch[f"{stage}_r_{group}"] = dma((partners - 1,))
 
     def row(values):
         return values.reshape(1, ROWS)
 
-    return pl.pallas_call(
-        functools.partial(kernel, nx, ny),
+    arguments = (
+        latent, row(move_to), row(move_slot), row(arrive_from), row(arrive_slot),
+        neighbours.T, row(valid_count), face_send.reshape(4, -1), corner_send.reshape(4, -1),
+        edge_in, edge_hid, node_in, node_out, biases.transpose(1, 0, 2), gains, grad_out,
+    )
+    for name, value in zip(ARGUMENTS, arguments):
+        scratch[name] = pltpu.VMEM(value.shape, value.dtype)
+    names = ["arg_" + name for name in ARGUMENTS] + list(RESULTS) + list(scratch)
+    state, grad_latent, early, late = pl.pallas_call(
+        functools.partial(kernel, nx, ny, names),
+        out_shape=(
+            shape((ROWS, D), BF16),
+            shape((ROWS, D), BF16),
+            shape((EARLY_ROWS, D), BF16),
+            shape((LATE_ROWS, D), BF16),
+        ),
+        in_specs=[pl.BlockSpec(memory_space=pl.ANY)] * len(ARGUMENTS),
+        out_specs=(vmem,) * len(RESULTS),
+        scratch_shapes=list(scratch.values()),
+        compiler_params=pltpu.CompilerParams(
+            collective_id=0, has_side_effects=True, vmem_limit_bytes=60 * 1024 * 1024
+        ),
+        name="evolve",
+    )(*arguments)
+    outputs = pl.pallas_call(
+        unpack,
         out_shape=(
             shape((ROWS, D), BF16),
             shape((ROWS, D), BF16),
@@ -588,21 +674,14 @@
             shape((LAYERS, 2, D, D), F32),
             shape((LAYERS, 2, D, D), F32),
             shape((LAYERS, D, D), F32),
-            shape((LAYERS, 5, D), F32),
+            shape((5, LAYERS, D), F32),
             shape((LAYERS, 2, D), F32),
         ),
-        in_specs=[vmem] * 16,
+        in_specs=[vmem] * 4,
         out_specs=(vmem,) * 8,
-        scratch_shapes=list(scratch.values()),
-        compiler_params=pltpu.CompilerParams(
-            collective_id=0, has_side_effects=True, vmem_limit_bytes=60 * 1024 * 1024
-        ),
-        name="evolve",
-    )(
-        latent, row(move_to), row(move_slot), row(arrive_from), row(arrive_slot),
-        neighbours.T, row(valid_count), face_send.reshape(4, -1), corner_send.reshape(4, -1),
-        edge_in, edge_hid, node_in, node_out, biases.transpose(1, 0, 2), gains, grad_out,
-    )
+        name="unpack",
+    )(state, grad_latent, early, late)
+    return *outputs[:6], outputs[6].transpose(1, 0, 2), outputs[7]
 
 
 def solution(mesh):

time: 88.6 us -> 78.4 us (0.88)
  local copies, waits for them, and re-layouts: 7.89 us -> 0 us
  Pallas kernels: 79.7 us -> 77.6 us
    unnamed x21 -> x0, local copies, waits for them, and re-layouts: 7.29 us -> none
    pallas_call x1 -> x2, Pallas kernels: 79.7 us -> 77.6 us  [the longest x1 75.4 us: shards(): pl.pallas_call(functools.partial(kernel, nx, ny, names), out_shape=(shape...]
where the time goes in v3:
time: 78.4 us; the launch traced here: 78.3 us
  Pallas kernels  77.6 us (99%)
    pallas_call x1, Pallas kernels, shards(): pl.pallas_call(functools.partial(kernel, nx, ny, names), out_shape=(shape...  75.4 us
    pallas_call x1, Pallas kernels, shards(): pl.pallas_call(unpack, out_shape=(shape((ROWS, D), BF16), shape((ROWS, D)...  2.18 us

profile of v3, /device:TPU:1, one launch (start us, length us, event | category | flops | bytes accessed | tf_op | source)
XLA Modules:
  0.0 78.3 jit_solution(8186874432354157392)
XLA Ops:
  0.6 75.4 %evolve.1 = (bf16[512,128]{1,0:T(8,128)(2,1)}, bf16[512,128]{1,0:T(8,128)(2,1)}, bf16[1280,128]{1,0:T(8,128)(2,1)}, bf16[768,128]{1,0:T(8,128)(2,1)}) custom-call(bf16[512,128]{1,0:T(8,128)(2,1)} %refs_0_.1, s32[1,512]{1,0:T(1,128)} %bitcast.12, s32[1,512]{1,0:T(1,128)} %bitcast.13, s32[1,512]{1,0:T(1,128)} %bitcast.14, s32[1,512]{1,0:T(1,128)} %bitcast.15, ...), custom_call_target="tpu_custom_call" | custom-call | tf_op jit(solution)/shard_map/evolve/pallas_call | solution.py:652
  76.1 2.2 %unpack.1 = (bf16[512,128]{1,0:T(8,128)(2,1)}, bf16[512,128]{1,0:T(8,128)(2,1)}, f32[2,2,128,128]{3,2,1,0:T(8,128)}, f32[2,2,128,128]{3,2,1,0:T(8,128)}, f32[2,2...) custom-call(bf16[512,128]{1,0:T(8,128)(2,1)} %get-tuple-element.20.state, ...), custom_call_target="tpu_custom_call" | custom-call | tf_op jit(solution)/shard_map/unpack/pallas_call | solution.py:668

commit v4 on v3

--- a/solution.py
+++ b/solution.py
@@ -13,7 +13,9 @@
 K = 16
 PAIRS = K // 2
 ROWS = 512
-HALF = 416
+HALF = 256
+HALO_HALF = 160
+PLACES = HALF + HALO_HALF
 HALO = 320
 CODES = 9
 SLOTS = CODES * CAP
@@ -47,7 +49,7 @@
 SCRATCH = (
     "outgoing", "arrived", "halo_out", "halo_in", "ret_out", "ret_in", "back_out", "back_in",
     "pick_send", "pick_back", "hits", "hits_t", "upper", "count_col", "state", "recv_term",
-    "send_tab", "w_mid", "w_out", "w_mid_t", "w_out_t", "ones", "h1s", "h2s", "d1s", "d2s", "xhs",
+    "own_tab", "halo_tab", "before", "w_mid", "w_out", "w_mid_t", "w_out_t", "ones", "h1s", "h2s", "d1s", "d2s", "xhs",
     "rss", "acc", "agg", "nhs", "d3s", "xh2s", "rs2s", "dxc", "g_recv", "agg_raw", "dsend",
     "dw_out", "dw_mid", "db_out", "db_mid", "mig_s", "mig_r", "halo_s", "halo_r", "ret_s", "ret_r",
     "back_s", "back_r",
@@ -130,11 +132,10 @@
         lat, move_to, move_slot, arrive_from, arrive_slot, nbr, count, face, corner,
         e_in, e_hid, n_in, n_out, bia, gai, gout,
     ) = (local for _, local in arguments)
-    state_o, glat_o, early_o, late_o = (refs[name] for name in RESULTS)
     (
         outgoing, arrived, halo_out, halo_in, ret_out, ret_in, back_out, back_in,
         pick_send, pick_back, hits, hits_t, upper, count_col,
-        state, recv_term, send_tab, w_mid, w_out, w_mid_t, w_out_t, ones,
+        state, recv_term, own_tab, halo_tab, before, w_mid, w_out, w_mid_t, w_out_t, ones,
         h1s, h2s, d1s, d2s, xhs, rss, acc, agg, nhs, d3s, xh2s, rs2s,
         dxc, g_recv, agg_raw, dsend, dw_out, dw_mid, db_out, db_mid,
         mig_s, mig_r, halo_s, halo_r, ret_s, ret_r, back_s, back_r,
@@ -213,6 +214,13 @@
             copy.wait_recv()
 
     everything = []
+    stored = []
+
+    def put_result(local, result):
+        copy = pltpu.make_async_copy(refs[local], refs[result], refs["store_s"].at[len(stored)])
+        copy.start()
+        stored.append(copy)
+
     migration = swap_slots(outgoing, arrived, mig_s, mig_r, 1)
     everything += migration
 
@@ -227,19 +235,26 @@
         pick_send[256 + index * 16 : 272 + index * 16, :] = one_hot_lanes(filled, ROWS)
     count_col[...] = column(as_row(count))
 
+    def placed(row):
+        halo = row - float(ROWS)
+        own_high = row >= float(HALF)
+        halo_high = halo >= float(HALO_HALF)
+        own_place = jnp.where(own_high, row - float(HALF), row)
+        halo_place = jnp.where(halo_high, halo - float(HALO_HALF), halo) + float(HALF)
+        own = row < float(ROWS)
+        high = jnp.where(own, jnp.where(own_high, 1.0, 0.0), jnp.where(halo_high, 1.0, 0.0))
+        return jnp.where(own, own_place, halo_place), high
+
     def build_hits(k, carry):
-        row = nbr[pl.ds(k, 1), :].astype(F32)
-        high = row >= float(HALF)
-        inner = jnp.where(high, row - float(HALF), row)
-        hits[k] = one_hot_lanes(column(inner), ROWS)
-        upper[k] = column(jnp.where(high, 1.0, 0.0))
+        place, high = placed(nbr[pl.ds(k, 1), :].astype(F32))
+        hits[k] = one_hot_lanes(column(place), ROWS)
+        upper[k] = column(high)
         return carry
 
     lax.fori_loop(0, K, build_hits, 0)
 
     def build_hits_t(k, carry):
-        row = nbr[pl.ds(k, 1), :].astype(F32)
-        hits_t[k] = one_hot_rows(jnp.where(row >= float(HALF), row - float(HALF), row), HALF)
+        hits_t[k] = one_hot_rows(placed(nbr[pl.ds(k, 1), :].astype(F32))[0], PLACES)
         return carry
 
     for load in loads[9:]:
@@ -259,7 +274,7 @@
         out = e_hid[layer, 1].astype(F32)
         w_mid[layer] = doubled(mid)
         w_out[layer] = doubled(out - jnp.mean(out, axis=1, keepdims=True))
-    send_tab[HALF:, :] = jnp.zeros((ROWS - HALF, 2 * D), BF16)
+    halo_tab[HALO_HALF:, :] = jnp.zeros((HALF - HALO_HALF, 2 * D), BF16)
 
     def bias(layer, index):
         return bia[index, layer : layer + 1, :]
@@ -287,22 +302,34 @@
         recv_term[...] = (dot(own, e_in[layer, 0]) + bias(layer, 0)) * 0.5
         w_send = (e_in[layer, 1].astype(F32) * 0.5).astype(BF16)
         own_send = dot(own, w_send).astype(BF16)
-        send_tab[0:HALF, 0:D] = own_send[0:HALF]
-        send_tab[0 : ROWS - HALF, D:] = own_send[HALF:]
+        own_tab[:, :D] = own_send[:HALF]
+        own_tab[:, D:] = own_send[HALF:]
         acc[...] = jnp.zeros((ROWS, D), F32)
         bias_mid = twice(bias(layer, 1)) * 0.5
         bias_out = bias(layer, 2)
         bias_out = twice(bias_out - jnp.mean(bias_out, axis=1, keepdims=True))
         meanwhile()
+
+        def own_chain(j, first):
+            rows = slice(first, first + BLOCK)
+            slots = (j, j + PAIRS)
+            both = [dot(hits[k, rows, :HALF], own_tab[...]) for k in slots]
+            yield
+            for k, pick in zip(slots, both):
+                before[k, rows] = recv_term[rows] + jnp.where(upper[k, rows] > 0.5, pick[:, D:], pick[:, :D])
+
+        staggered(own_chain, 4)
         landed(halo)
-        send_tab[ROWS - HALF : HALF, D:] = dot(halo_in[layer], w_send).astype(BF16)
+        halo_send = dot(halo_in[layer], w_send).astype(BF16)
+        halo_tab[:HALO_HALF, :D] = halo_send[:HALO_HALF]
+        halo_tab[:HALO_HALF, D:] = halo_send[HALO_HALF:]
 
         def chain(j, first):
             rows = slice(first, first + BLOCK)
-            both = [dot(hits[k, rows], send_tab[...]) for k in (j, j + PAIRS)]
+            both = [dot(hits[k, rows, HALF:], halo_tab[...]) for k in (j, j + PAIRS)]
             yield
             parts = [
-                recv_term[rows] + jnp.where(upper[k, rows] > 0.5, pick[:, D:], pick[:, :D])
+                before[k, rows] + jnp.where(upper[k, rows] > 0.5, pick[:, D:], pick[:, :D])
                 for k, pick in zip((j, j + PAIRS), both)
             ]
             value, slope = half_silu(jnp.concatenate(parts, axis=1))
@@ -350,7 +377,8 @@
         if layer + 1 < LAYERS:
             state[layer + 1] = following
         else:
-            state_o[...] = following
+            refs["state_v"][...] = following
+            put_result("state_v", "state_o")
 
     def put_term(group, index, values):
         refs["terms_" + group][index * D : index * D + D, :] = values.astype(BF16)
@@ -431,12 +459,18 @@
         lifted = grad_agg * gain(layer, 0)
         dxc[...] = lifted - jnp.mean(lifted, axis=1, keepdims=True)
         g_recv[...] = jnp.zeros((ROWS, D), F32)
-        dsend[...] = jnp.zeros((HALF, 2 * D), F32)
+        dsend[...] = jnp.zeros((PLACES, 2 * D), F32)
         dw_out[...] = jnp.zeros((D, D), F32)
         dw_mid[...] = jnp.zeros((D, D), F32)
         db_out[...] = jnp.zeros((8, 2 * D), F32)
         db_mid[...] = jnp.zeros((8, 2 * D), F32)
         before_edges()
+
+        later = layer == LAYERS - 1
+        lowest = HALF if later else 0
+
+        def add_hidden(total, hidden, grad):
+            total[...] += dot_tn(hidden[:, :D], grad[:, :D]) + dot_tn(hidden[:, D:], grad[:, D:])
 
         def chain(j, first):
             rows = slice(first, first + BLOCK)
@@ -448,15 +482,19 @@
             db_out[...] += partial_sums(grad)
             grad = grad.astype(BF16)
             product = dot(grad, w_out_t[layer])
-            hidden = h2s[layer, j, rows]
-            dw_out[...] += dot_tn(hidden[:, :D], grad[:, :D]) + dot_tn(hidden[:, D:], grad[:, D:])
+            if later:
+                hits[j, rows, HALF:] = grad
+            else:
+                add_hidden(dw_out, h2s[layer, j, rows], grad)
             yield
             grad = product * d2s[layer, j, rows].astype(F32)
             db_mid[...] += partial_sums(grad)
             grad = grad.astype(BF16)
             product = dot(grad, w_mid_t[layer])
-            hidden = h1s[layer, j, rows]
-            dw_mid[...] += dot_tn(hidden[:, :D], grad[:, :D]) + dot_tn(hidden[:, D:], grad[:, D:])
+            if later:
+                hits[j + PAIRS, rows, HALF:] = grad
+            else:
+                add_hidden(dw_mid, h1s[layer, j, rows], grad)
             yield
             grad = product * d1s[layer, j, rows].astype(F32)
             g_recv[rows] += grad[:, :D] + grad[:, D:]
@@ -466,20 +504,32 @@
                 piece = grad[:, part * D : part * D + D]
                 high = upper[k, rows] > 0.5
                 split = jnp.concatenate([jnp.where(high, 0.0, piece), jnp.where(high, piece, 0.0)], axis=1)
-                added = dot(hits_t[k, :, rows], split.astype(BF16))
+                split = split.astype(BF16)
+                if later:
+                    hits[k, rows, :HALF] = split
+                added = dot(hits_t[k, lowest:, rows], split)
                 scattered = added if scattered is None else scattered + added
-            dsend[...] += scattered
+            dsend[lowest:] += scattered
 
         staggered(chain, BACKWARD_PAIRS)
-        send_grad = dsend[...].astype(BF16)
-        low = send_grad[:, :D]
-        high_own = send_grad[: ROWS - HALF, D:]
-        high_halo = send_grad[ROWS - HALF :, D:]
-        ret_out[layer] = dot_nt(high_halo, e_in[layer, 1]).astype(BF16)
+        halo_grad = dsend[HALF:].astype(BF16)
+        halo_grad = jnp.concatenate([halo_grad[:, :D], halo_grad[:, D:]], axis=0)
+        ret_out[layer] = dot_nt(halo_grad, e_in[layer, 1]).astype(BF16)
         returning = swap_halo(ret_out.at[layer], ret_in.at[layer], ret_s.at[layer], ret_r.at[layer], -1)
         everything.extend(returning)
-        send_own = jnp.concatenate([low, high_own], axis=0)
-        term = dot_tn(own, send_own) + dot_tn(halo_in[layer], high_halo)
+        if later:
+
+            def rest(j, first):
+                rows = slice(first, first + BLOCK)
+                dsend[:HALF] += sum(dot(hits_t[k, :HALF, rows], hits[k, rows, :HALF]) for k in (j, j + PAIRS))
+                add_hidden(dw_out, h2s[layer, j, rows], hits[j, rows, HALF:])
+                add_hidden(dw_mid, h1s[layer, j, rows], hits[j + PAIRS, rows, HALF:])
+                yield
+
+            staggered(rest, 2)
+        send_own = dsend[:HALF].astype(BF16)
+        send_own = jnp.concatenate([send_own[:, :D], send_own[:, D:]], axis=0)
+        term = dot_tn(own, send_own) + dot_tn(halo_in[layer], halo_grad)
         group = EDGE_GROUPS[layer]
         put_term(group, 1, term)
         grad = g_recv[...]
@@ -531,12 +581,15 @@
     staying = dot(stay_pick, rounded)
     sums["early"] = spread_start("early", sums["early"])
     landed(going_back)
-    glat_o[...] = (staying + dot(come_pick, back_in[...])).astype(BF16)
+    refs["glat_v"][...] = (staying + dot(come_pick, back_in[...])).astype(BF16)
+    put_result("glat_v", "glat_o")
     sums["late"] = spread_start("late", sums["late"])
     landed(sums["early"])
-    early_o[...] = refs["final_early"][...].reshape(EARLY_ROWS, D)
+    put_result("final_early", "early_o")
     landed(sums["late"])
-    late_o[...] = refs["final_late"][...].reshape(LATE_ROWS, D)
+    put_result("final_late", "late_o")
+    for copy in stored:
+        copy.wait()
     for copy in everything:
         copy.wait_send()
 
@@ -587,12 +640,14 @@
         pick_send=pltpu.VMEM((HALO, ROWS), BF16),
         pick_back=pltpu.VMEM((ROWS, HALO), BF16),
         hits=pltpu.VMEM((K, ROWS, ROWS), BF16),
-        hits_t=pltpu.VMEM((K, HALF, ROWS), BF16),
+        hits_t=pltpu.VMEM((K, PLACES, ROWS), BF16),
         upper=pltpu.VMEM((K, ROWS, D), F32),
         count_col=pltpu.VMEM((ROWS, D), F32),
         state=node_bf,
         recv_term=pltpu.VMEM((ROWS, D), F32),
-        send_tab=pltpu.VMEM((ROWS, 2 * D), BF16),
+        own_tab=pltpu.VMEM((HALF, 2 * D), BF16),
+        halo_tab=pltpu.VMEM((HALF, 2 * D), BF16),
+        before=pltpu.VMEM((K, ROWS, D), F32),
         w_mid=wide,
         w_out=wide,
         w_mid_t=wide,
@@ -613,7 +668,7 @@
         dxc=pltpu.VMEM((ROWS, D), F32),
         g_recv=pltpu.VMEM((ROWS, D), F32),
         agg_raw=node,
-        dsend=pltpu.VMEM((HALF, 2 * D), F32),
+        dsend=pltpu.VMEM((PLACES, 2 * D), F32),
         dw_out=pltpu.VMEM((D, D), F32),
         dw_mid=pltpu.VMEM((D, D), F32),
         db_out=pltpu.VMEM((8, 2 * D), F32),
@@ -627,6 +682,9 @@
         back_s=dma((CODES,)),
         back_r=dma((CODES,)),
         load_s=dma((16,)),
+        store_s=dma((4,)),
+        state_v=pltpu.VMEM((ROWS, D), BF16),
+        glat_v=pltpu.VMEM((ROWS, D), BF16),
     )
     for group, total in (("early", EARLY_ROWS), ("late", LATE_ROWS)):
         chunk = total // ny
@@ -654,14 +712,14 @@
         out_shape=(
             shape((ROWS, D), BF16),
             shape((ROWS, D), BF16),
-            shape((EARLY_ROWS, D), BF16),
-            shape((LATE_ROWS, D), BF16),
+            shape((ny, EARLY_ROWS // ny, D), BF16),
+            shape((ny, LATE_ROWS // ny, D), BF16),
         ),
         in_specs=[pl.BlockSpec(memory_space=pl.ANY)] * len(ARGUMENTS),
-        out_specs=(vmem,) * len(RESULTS),
+        out_specs=(pl.BlockSpec(memory_space=pl.ANY),) * len(RESULTS),
         scratch_shapes=list(scratch.values()),
         compiler_params=pltpu.CompilerParams(
-            collective_id=0, has_side_effects=True, vmem_limit_bytes=60 * 1024 * 1024
+            collective_id=0, has_side_effects=True, vmem_limit_bytes=62 * 1024 * 1024
         ),
         name="evolve",
     )(*arguments)
@@ -680,7 +738,7 @@
         in_specs=[vmem] * 4,
         out_specs=(vmem,) * 8,
         name="unpack",
-    )(state, grad_latent, early, late)
+    )(state, grad_latent, early.reshape(EARLY_ROWS, D), late.reshape(LATE_ROWS, D))
     return *outputs[:6], outputs[6].transpose(1, 0, 2), outputs[7]
 
 

time: 78.4 us -> 74.8 us (0.954)
  Pallas kernels: 77.6 us -> 74 us
    pallas_call x1, Pallas kernels: 75.4 us -> 71.8 us  [shards(): pl.pallas_call(functools.partial(kernel, nx, ny, names), out_shape=(shape...]
where the time goes in v4:
time: 74.8 us; the launch traced here: 74.6 us
  Pallas kernels  74 us (99%)
    pallas_call x1, Pallas kernels, shards(): pl.pallas_call(functools.partial(kernel, nx, ny, names), out_shape=(shape...  71.8 us
    pallas_call x1, Pallas kernels, shards(): pl.pallas_call(unpack, out_shape=(shape((ROWS, D), BF16), shape((ROWS, D)...  2.18 us

profile of v4, /device:TPU:1, one launch (start us, length us, event | category | flops | bytes accessed | tf_op | source)
XLA Modules:
  0.0 74.6 jit_solution(13559395204029957784)
XLA Ops:
  0.6 71.8 %evolve.1 = (bf16[512,128]{1,0:T(8,128)(2,1)}, bf16[512,128]{1,0:T(8,128)(2,1)}, bf16[16,80,128]{2,1,0:T(8,128)(2,1)}, bf16[16,48,128]{2,1,0:T(8,128)(2,1)}) custom-call(bf16[512,128]{1,0:T(8,128)(2,1)} %refs_0_.1, s32[1,512]{1,0:T(1,128)} %bitcast.16, s32[1,512]{1,0:T(1,128)} %bitcast.17, s32[1,512]{1,0:T(1,128)} %bitcast.18, s32[1,512]{1,0:T(1,128)} %bitcast.19, ...), custom_call_target="tpu_custom_call" | custom-call | tf_op jit(solution)/shard_map/evolve/pallas_call | solution.py:710
  72.4 2.2 %unpack.1 = (bf16[512,128]{1,0:T(8,128)(2,1)}, bf16[512,128]{1,0:T(8,128)(2,1)}, f32[2,2,128,128]{3,2,1,0:T(8,128)}, f32[2,2,128,128]{3,2,1,0:T(8,128)}, f32[2,2...) custom-call(bf16[512,128]{1,0:T(8,128)(2,1)} %get-tuple-element.20.state, ...), custom_call_target="tpu_custom_call" | custom-call | tf_op jit(solution)/shard_map/unpack/pallas_call | solution.py:726

commit v5 on v4

--- a/solution.py
+++ b/solution.py
@@ -110,6 +110,11 @@
     lax.fori_loop(0, PAIRS // pairs, body, 0)
 
 
+def far_first(copies):
+    middle = (len(copies) - 1) / 2
+    return [copies[index] for index in sorted(range(len(copies)), key=lambda index: abs(index - middle))]
+
+
 def layer_norm_parts(values):
     centred = values - jnp.mean(values, axis=1, keepdims=True)
     scale = lax.rsqrt(jnp.mean(centred * centred, axis=1, keepdims=True) + 1e-05)
@@ -117,6 +122,7 @@
 
 
 def half_silu(half):
+    half = half.astype(BF16)
     wave = jnp.tanh(half)
     gate = 1.0 + wave
     value = half * gate
@@ -180,20 +186,18 @@
     pl.semaphore_wait(barrier, len(partners))
 
     def swap_slots(source, target, send, recv, sign):
-        copies = []
+        copies = {}
         for code, (move_x, move_y) in enumerate(TRAVEL):
             if code == 4:
                 continue
             rows = pl.ds(code * CAP, CAP)
-            copies.append(
-                remote(
-                    source.at[rows], target.at[rows], send.at[code], recv.at[code],
-                    at(sign * move_x, sign * move_y),
-                )
+            copies[code] = remote(
+                source.at[rows], target.at[rows], send.at[code], recv.at[code],
+                at(sign * move_x, sign * move_y),
             )
-        for copy in copies:
-            copy.start()
-        return copies
+        for code in (0, 2, 6, 8, 1, 7, 3, 5):
+            copies[code].start()
+        return list(copies.values())
 
     def swap_halo(source, target, send, recv, sign):
         copies = []
@@ -205,7 +209,7 @@
                     at(sign * move_x, sign * move_y),
                 )
             )
-        for copy in copies:
+        for copy in copies[4:] + copies[:4]:
             copy.start()
         return copies
 
@@ -366,7 +370,7 @@
         value, slope = half_silu(half)
         value = value.astype(BF16)
         nhs[layer] = value
-        d3s[layer] = slope
+        d3s[layer] = slope.astype(F32)
         normed, scale = layer_norm_parts(dot(value, n_out[layer]) + bias(layer, 4))
         xh2s[layer] = normed
         rs2s[layer] = jnp.broadcast_to(scale, (ROWS, D))
@@ -392,7 +396,7 @@
             rows = pl.ds(pl.multiple_of(peer * chunk, chunk), chunk)
             sems = (refs["rs_s_" + group].at[step - 1], refs["rs_r_" + group].at[step - 1])
             copies.append(remote(terms.at[rows], arriving.at[step - 1], *sems, (a, peer)))
-        for copy in copies:
+        for copy in far_first(copies):
             copy.start()
         everything.extend(copies)
         return copies
@@ -412,7 +416,7 @@
             sems = (refs["ar_s_" + group].at[step - 1], refs["ar_r_" + group].at[step - 1])
             out.append(remote(summed.at[a], summed.at[a], *sems, (peer, b)))
             come.append(remote(summed.at[source], summed.at[source], *sems, (peer, b)))
-        for copy in out:
+        for copy in far_first(out):
             copy.start()
         everything.extend(out)
         return come
@@ -431,14 +435,14 @@
             sems = (refs["ag_s_" + group].at[step - 1], refs["ag_r_" + group].at[step - 1])
             out.append(remote(final.at[b], final.at[b], *sems, (a, peer)))
             come.append(remote(final.at[source], final.at[source], *sems, (a, peer)))
-        for copy in out:
+        for copy in far_first(out):
             copy.start()
         everything.extend(out)
         return come
 
     vectors = []
 
-    def backward(layer, cotangent, before_edges, after_terms):
+    def backward(layer, cotangent, before_edges):
         own = state[layer]
         normed = xh2s[layer]
         lifted = cotangent * gain(layer, 1)
@@ -514,10 +518,15 @@
         staggered(chain, BACKWARD_PAIRS)
         halo_grad = dsend[HALF:].astype(BF16)
         halo_grad = jnp.concatenate([halo_grad[:, :D], halo_grad[:, D:]], axis=0)
-        ret_out[layer] = dot_nt(halo_grad, e_in[layer, 1]).astype(BF16)
-        returning = swap_halo(ret_out.at[layer], ret_in.at[layer], ret_s.at[layer], ret_r.at[layer], -1)
-        everything.extend(returning)
+
+        def send_back():
+            ret_out[layer] = dot_nt(halo_grad, e_in[layer, 1]).astype(BF16)
+            copies = swap_halo(ret_out.at[layer], ret_in.at[layer], ret_s.at[layer], ret_r.at[layer], -1)
+            everything.extend(copies)
+            return copies
+
         if later:
+            returning = send_back()
 
             def rest(j, first):
                 rows = slice(first, first + BLOCK)
@@ -549,8 +558,12 @@
             grad_gain_edge,
             grad_gain_node,
         ])
-        after_terms()
+        if not later:
+            late_start()
+            returning = send_back()
         own_grad = own_grad + dot_nt(grad, e_in[layer, 0]) + dot_nt(send_own, e_in[layer, 1])
+        if not later:
+            prepare_end()
         landed(returning)
         own_grad = own_grad + dot(pick_back[...], ret_in[layer])
         return own_grad.astype(BF16)
@@ -566,24 +579,27 @@
         stacked = jnp.concatenate(vectors + [jnp.zeros((2, D), F32)], axis=0)
         terms[LATE_VECTORS : LATE_VECTORS + 16, :] = stacked.astype(BF16)
         sums["late"] = reduce_start("late")
+
+    def prepare_end():
         sums["early"] = exchange_start("early", sums["early"])
-
-    rounded = backward(1, gout[...].astype(F32), lambda: None, lambda: None)
-    rounded = backward(0, rounded.astype(F32), early_start, late_start)
-
-    back_target = jnp.where(from_row == 4.0, -1.0, from_row * CAP + aslot_row)
-    back_out[...] = dot(one_hot_rows(back_target, SLOTS), rounded).astype(BF16)
+        back_target = jnp.where(from_row == 4.0, -1.0, from_row * CAP + aslot_row)
+        hits[0, :SLOTS, :] = one_hot_rows(back_target, SLOTS)
+        hits[1] = one_hot_lanes(column(jnp.where(to_row == 4.0, slot_row, -1.0)), ROWS)
+        hits[2, :, :POOL] = one_hot_lanes(column(out_target), POOL)
+        sums["late"] = exchange_start("late", sums["late"])
+
+    rounded = backward(1, gout[...].astype(F32), lambda: None)
+    rounded = backward(0, rounded.astype(F32), early_start)
+
+    back_out[...] = dot(hits[0, :SLOTS, :], rounded).astype(BF16)
     going_back = swap_slots(back_out, back_in, back_s, back_r, -1)
     everything += going_back
-    sums["late"] = exchange_start("late", sums["late"])
-    stay_pick = one_hot_lanes(column(jnp.where(to_row == 4.0, slot_row, -1.0)), ROWS)
-    come_pick = one_hot_lanes(column(out_target), POOL)
-    staying = dot(stay_pick, rounded)
+    staying = dot(hits[1], rounded)
     sums["early"] = spread_start("early", sums["early"])
+    sums["late"] = spread_start("late", sums["late"])
     landed(going_back)
-    refs["glat_v"][...] = (staying + dot(come_pick, back_in[...])).astype(BF16)
+    refs["glat_v"][...] = (staying + dot(hits[2, :, :POOL], back_in[...])).astype(BF16)
     put_result("glat_v", "glat_o")
-    sums["late"] = spread_start("late", sums["late"])
     landed(sums["early"])
     put_result("final_early", "early_o")
     landed(sums["late"])

time: 74.8 us -> 73.9 us (0.988)
  Pallas kernels: 74 us -> 73.1 us
    pallas_call x1, Pallas kernels: 71.8 us -> 70.9 us  [shards(): pl.pallas_call(functools.partial(kernel, nx, ny, names), out_shape=(shape...]
where the time goes in v5:
time: 73.9 us; the launch traced here: 73.7 us
  Pallas kernels  73.1 us (99%)
    pallas_call x1, Pallas kernels, shards(): pl.pallas_call(functools.partial(kernel, nx, ny, names), out_shape=(shape...  70.9 us
    pallas_call x1, Pallas kernels, shards(): pl.pallas_call(unpack, out_shape=(shape((ROWS, D), BF16), shape((ROWS, D)...  2.18 us

profile of v5, /device:TPU:1, one launch (start us, length us, event | category | flops | bytes accessed | tf_op | source)
XLA Modules:
  0.0 73.7 jit_solution(15394633247577901287)
XLA Ops:
  0.6 70.9 %evolve.1 = (bf16[512,128]{1,0:T(8,128)(2,1)}, bf16[512,128]{1,0:T(8,128)(2,1)}, bf16[16,80,128]{2,1,0:T(8,128)(2,1)}, bf16[16,48,128]{2,1,0:T(8,128)(2,1)}) custom-call(bf16[512,128]{1,0:T(8,128)(2,1)} %refs_0_.1, s32[1,512]{1,0:T(1,128)} %bitcast.16, s32[1,512]{1,0:T(1,128)} %bitcast.17, s32[1,512]{1,0:T(1,128)} %bitcast.18, s32[1,512]{1,0:T(1,128)} %bitcast.19, ...), custom_call_target="tpu_custom_call" | custom-call | tf_op jit(solution)/shard_map/evolve/pallas_call | solution.py:726
  71.6 2.2 %unpack.1 = (bf16[512,128]{1,0:T(8,128)(2,1)}, bf16[512,128]{1,0:T(8,128)(2,1)}, f32[2,2,128,128]{3,2,1,0:T(8,128)}, f32[2,2,128,128]{3,2,1,0:T(8,128)}, f32[2,2...) custom-call(bf16[512,128]{1,0:T(8,128)(2,1)} %get-tuple-element.20.state, ...), custom_call_target="tpu_custom_call" | custom-call | tf_op jit(solution)/shard_map/unpack/pallas_call | solution.py:742

commit v6 on v5

--- a/solution.py
+++ b/solution.py
@@ -110,11 +110,6 @@
     lax.fori_loop(0, PAIRS // pairs, body, 0)
 
 
-def far_first(copies):
-    middle = (len(copies) - 1) / 2
-    return [copies[index] for index in sorted(range(len(copies)), key=lambda index: abs(index - middle))]
-
-
 def layer_norm_parts(values):
     centred = values - jnp.mean(values, axis=1, keepdims=True)
     scale = lax.rsqrt(jnp.mean(centred * centred, axis=1, keepdims=True) + 1e-05)
@@ -195,7 +190,7 @@
                 source.at[rows], target.at[rows], send.at[code], recv.at[code],
                 at(sign * move_x, sign * move_y),
             )
-        for code in (0, 2, 6, 8, 1, 7, 3, 5):
+        for code in (0, 1, 2, 3, 5, 6, 7, 8):
             copies[code].start()
         return list(copies.values())
 
@@ -209,7 +204,7 @@
                     at(sign * move_x, sign * move_y),
                 )
             )
-        for copy in copies[4:] + copies[:4]:
+        for copy in copies:
             copy.start()
         return copies
 
@@ -396,7 +391,7 @@
             rows = pl.ds(pl.multiple_of(peer * chunk, chunk), chunk)
             sems = (refs["rs_s_" + group].at[step - 1], refs["rs_r_" + group].at[step - 1])
             copies.append(remote(terms.at[rows], arriving.at[step - 1], *sems, (a, peer)))
-        for copy in far_first(copies):
+        for copy in copies:
             copy.start()
         everything.extend(copies)
         return copies
@@ -416,7 +411,7 @@
             sems = (refs["ar_s_" + group].at[step - 1], refs["ar_r_" + group].at[step - 1])
             out.append(remote(summed.at[a], summed.at[a], *sems, (peer, b)))
             come.append(remote(summed.at[source], summed.at[source], *sems, (peer, b)))
-        for copy in far_first(out):
+        for copy in out:
             copy.start()
         everything.extend(out)
         return come
@@ -435,7 +430,7 @@
             sems = (refs["ag_s_" + group].at[step - 1], refs["ag_r_" + group].at[step - 1])
             out.append(remote(final.at[b], final.at[b], *sems, (a, peer)))
             come.append(remote(final.at[source], final.at[source], *sems, (a, peer)))
-        for copy in far_first(out):
+        for copy in out:
             copy.start()
         everything.extend(out)
         return come

time: 73.9 us -> 73 us (0.988)
  Pallas kernels: 73.1 us -> 72.2 us
    pallas_call x1, Pallas kernels: 70.9 us -> 70 us  [shards(): pl.pallas_call(functools.partial(kernel, nx, ny, names), out_shape=(shape...]
where the time goes in v6:
time: 73 us; the launch traced here: 72.9 us
  Pallas kernels  72.2 us (99%)
    pallas_call x1, Pallas kernels, shards(): pl.pallas_call(functools.partial(kernel, nx, ny, names), out_shape=(shape...  70 us
    pallas_call x1, Pallas kernels, shards(): pl.pallas_call(unpack, out_shape=(shape((ROWS, D), BF16), shape((ROWS, D)...  2.18 us

profile of v6, /device:TPU:1, one launch (start us, length us, event | category | flops | bytes accessed | tf_op | source)
XLA Modules:
  0.0 72.9 jit_solution(16247626603521883508)
XLA Ops:
  0.6 70.0 %evolve.1 = (bf16[512,128]{1,0:T(8,128)(2,1)}, bf16[512,128]{1,0:T(8,128)(2,1)}, bf16[16,80,128]{2,1,0:T(8,128)(2,1)}, bf16[16,48,128]{2,1,0:T(8,128)(2,1)}) custom-call(bf16[512,128]{1,0:T(8,128)(2,1)} %refs_0_.1, s32[1,512]{1,0:T(1,128)} %bitcast.16, s32[1,512]{1,0:T(1,128)} %bitcast.17, s32[1,512]{1,0:T(1,128)} %bitcast.18, s32[1,512]{1,0:T(1,128)} %bitcast.19, ...), custom_call_target="tpu_custom_call" | custom-call | tf_op jit(solution)/shard_map/evolve/pallas_call | solution.py:721
  70.7 2.2 %unpack.1 = (bf16[512,128]{1,0:T(8,128)(2,1)}, bf16[512,128]{1,0:T(8,128)(2,1)}, f32[2,2,128,128]{3,2,1,0:T(8,128)}, f32[2,2,128,128]{3,2,1,0:T(8,128)}, f32[2,2...) custom-call(bf16[512,128]{1,0:T(8,128)(2,1)} %get-tuple-element.20.state, ...), custom_call_target="tpu_custom_call" | custom-call | tf_op jit(solution)/shard_map/unpack/pallas_call | solution.py:737
